TPU v7x, 32 devices: a whole 2x2x4 slice. The times are simulated.
32 devices in a mesh: gx: 4 (over y, core), gy: 2 (over x), gz: 4 (over z).
Axes of the slice: x: 2, y: 2, z: 4, core: 2. Of those that a mesh axis runs over, the one named last changes fastest.
Arguments:
- trial: bfloat16 [8, 4, 16, 64, 128], P('gx', 'gy', 'gz'), may hold values from -6 to 6
- onsite: bfloat16 [8, 4, 16, 128, 128], P('gx', 'gy', 'gz'), as said below
- coupling: bfloat16 [3, 8, 4, 16, 128, 128], P(None, 'gx', 'gy', 'gz'), may hold values from -0.1875 to 0.1875
- bonds: int32 [3, 8, 4, 16], P(None, 'gx', 'gy', 'gz'), may hold values 0 or 1
Outputs:
- filtered: float32 [8, 4, 16, 64, 128], P('gx', 'gy', 'gz')
Inputs may be any that keep to these rules, and one draw needn't show every extreme that they name: `onsite`: each on-site block is symmetric in its last two dimensions.
All inputs are finite; a program needn't handle non-finite values. No bound on the sum of `bonds` on one device may be relied on, other than what follows from the above.
Results may differ from a plain program's by a relative error of at most 0.0052.
Values may be sent and summed in bfloat16 or wider, within the bound.
A program may use at most 64 MiB of HBM per device.

v0:
```python
import jax
import jax.numpy as jnp
from jax import lax
from jax.sharding import PartitionSpec as P

STEPS = 5


center_shift = 0.25
half_inverse = 0.5


def passed_along(block, axis, distance):
    devices = range(lax.axis_size(axis))
    route = [(i - distance, i) for i in devices if i - distance in devices]
    return lax.ppermute(block, axis, route)


def block_apply(blocks, vecs):
    return jnp.einsum("...pq,...kq->...kp", blocks, vecs, preferred_element_type=jnp.float32)


def block_transposed(blocks, vecs):
    return jnp.einsum("...pq,...kp->...kq", blocks, vecs, preferred_element_type=jnp.float32)


def layer_of(array, axis, start, count):
    return lax.slice_in_dim(array, start, start + count, axis=axis)


def add_layers(total, axis, start, count, term):
    index = [slice(None)] * total.ndim
    index[axis] = slice(start, start + count)
    return total.at[tuple(index)].add(term)


def interior_terms(onsite, blocks, vecs):
    total = block_apply(onsite, vecs)
    for axis in range(3):
        length = vecs.shape[axis]
        own_blocks = layer_of(blocks[axis], axis, 0, length - 1)
        forward = block_apply(own_blocks, layer_of(vecs, axis, 1, length - 1))
        total = add_layers(total, axis, 0, length - 1, forward)
        backward = block_transposed(own_blocks, layer_of(vecs, axis, 0, length - 1))
        total = add_layers(total, axis, 1, length - 1, backward)
    return total


def returned_terms(onsite, blocks, vecs):
    lengths = (vecs.shape[0], vecs.shape[1], vecs.shape[2])
    tops = []
    upwards = []
    for axis in range(3):
        top_blocks = layer_of(blocks[axis], axis, lengths[axis] - 1, 1)
        tops.append(top_blocks)
        upwards.append(block_transposed(top_blocks, layer_of(vecs, axis, lengths[axis] - 1, 1)))
    above_x = passed_along(layer_of(vecs, 0, 0, 1), "gx", -1)
    above_y = passed_along(layer_of(vecs, 1, 0, 1), "gy", -1)
    above_z = passed_along(layer_of(vecs, 2, 0, 1), "gz", -1)
    below_x = passed_along(upwards[0], "gx", 1)
    below_y = passed_along(upwards[1], "gy", 1)
    below_z = passed_along(upwards[2], "gz", 1)
    above = (above_x, above_y, above_z)
    below = (below_x, below_y, below_z)
    total = interior_terms(onsite, blocks, vecs)
    for axis in range(3):
        total = add_layers(total, axis, lengths[axis] - 1, 1, block_apply(tops[axis], above[axis]))
        total = add_layers(total, axis, 0, 1, below[axis])
    return total


def shards(trial, onsite, coupling, bonds):
    blocks = coupling * bonds.astype(jnp.bfloat16)[..., None, None]

    def apply_operator(vecs):
        return returned_terms(onsite, blocks, vecs)

    def scaled(vecs):
        return half_inverse * (apply_operator(vecs) - center_shift * vecs.astype(jnp.float32))

    previous = trial
    current = scaled(trial).astype(jnp.bfloat16)
    for step in range(STEPS - 2):
        following = (2.0 * scaled(current) - previous.astype(jnp.float32)).astype(jnp.bfloat16)
        previous = current
        current = following
    return 2.0 * scaled(current) - previous.astype(jnp.float32)


def solution(mesh):
    placed = (
        P("gx", "gy", "gz", None, None),
        P("gx", "gy", "gz", None, None),
        P(None, "gx", "gy", "gz", None, None),
        P(None, "gx", "gy", "gz"),
    )
    return jax.shard_map(
        shards,
        mesh=mesh,
        in_specs=placed,
        out_specs=P("gx", "gy", "gz", None, None),
        check_vma=False,
    )
```

profile of v0, /device:TPU:0, one launch (start us, length us, event | category | flops | bytes accessed | tf_op | source)
XLA Modules:
  0.0 118.7 jit_solution(3793378843484865508)
XLA Ops:
  0.0 1.0 slice.2264
  1.0 1.3 %collective-permute-start = (bf16[1,2,4,64,128]{4,3,2,1,0:T(8,128)(2,1)S(1)}, bf16[1,2,4,64,128]{4,3,2,1,0:T(8,128)(2,1)S(1)}, u32[]{:S(2)}, u32[]{:S(2)}) collective-permute-start(bf16[1,2,4,64,128]{4,3,2,1,0:T(8,128)(2,1)S(1)} %slice.2264), channel_id=1, source_target_pairs={{8,0},{16,8},{24,16},{9,1},{17,9},{25,17},{10,2},{18,10},{26,18},{... | collective-permute-start | bytes 393224 | tf_op jit(solution)/shard_map/ppermute | solution.py:16
  2.3 0.7 convert_element_type.34
  3.0 1.6 %broadcast_multiply_fusion = bf16[3,2,2,4,128,128]{5,4,3,2,1,0:T(8,128)(2,1)S(1)} fusion(bf16[3,2,2,4,128,128]{5,4,3,2,1,0:T(8,128)(2,1)} %param.126, bf16[3,2,2,4]{3,2,1,0:T(2,128)(2,1)S(1)} %convert_element_type.34), kind=kLoop, calls=%fused_computation.122 | loop fusion | flops 786432 | bytes 3145824 | tf_op jit(solution)/shard_map/mul | solution.py:73
  4.8 3.0 %collective-permute-start.1 = (f32[1,2,4,64,128]{4,3,2,1,0:T(8,128)S(1)}, f32[1,2,4,64,128]{4,3,2,1,0:T(8,128)S(1)}, u32[]{:S(2)}, u32[]{:S(2)}) collective-permute-start(f32[1,2,4,64,128]{4,3,2,1,0:T(8,128)S(1)} %convolution_bitcast_fusion.3), channel_id=1, source_target_pairs={{0,8},{8,16},{16,24},{1,9},{9,17},{17,25},{2,10},{10,18},{18,26},{... | collective-permute-start | bytes 786440 | tf_op jit(solution)/shard_map/ppermute | solution.py:16
  7.9 1.3 %collective-permute-start.2 = (bf16[2,1,4,64,128]{4,3,2,0,1:T(8,128)(2,1)S(1)}, bf16[2,1,4,64,128]{4,3,2,0,1:T(8,128)(2,1)S(1)}, u32[]{:S(2)}, u32[]{:S(2)}) collective-permute-start(bf16[2,1,4,64,128]{4,3,2,0,1:T(8,128)(2,1)S(1)} %slice_bitcast_fusion.31), channel_id=1, source_target_pairs={{4,0},{5,1},{6,2},{7,3},{12,8},{13,9},{14,10},{15,11},{20,16},{21,... | collective-permute-start | bytes 393224 | tf_op jit(solution)/shard_map/ppermute | solution.py:16
  9.5 4.9 %collective-permute-start.3 = (f32[2,1,4,64,128]{4,3,2,1,0:T(8,128)S(1)}, f32[2,1,4,64,128]{4,3,2,1,0:T(8,128)S(1)}, u32[]{:S(2)}, u32[]{:S(2)}) collective-permute-start(f32[2,1,4,64,128]{4,3,2,1,0:T(8,128)S(1)} %convolution_bitcast_fusion.2), channel_id=1, source_target_pairs={{0,4},{1,5},{2,6},{3,7},{8,12},{9,13},{10,14},{11,15},{16,20},{17,... | collective-permute-start | bytes 786440 | tf_op jit(solution)/shard_map/ppermute | solution.py:16
  14.3 1.3 %collective-permute-start.4 = (bf16[2,2,1,64,128]{4,3,1,0,2:T(8,128)(2,1)S(1)}, bf16[2,2,1,64,128]{4,3,1,0,2:T(8,128)(2,1)S(1)}, u32[]{:S(2)}, u32[]{:S(2)}) collective-permute-start(bf16[2,2,1,64,128]{4,3,1,0,2:T(8,128)(2,1)S(1)} %slice_bitcast_fusion.40), channel_id=1, source_target_pairs={{1,0},{2,1},{3,2},{5,4},{6,5},{7,6},{9,8},{10,9},{11,10},{13,12},{... | collective-permute-start | bytes 196616 | tf_op jit(solution)/shard_map/ppermute | solution.py:16
  15.7 0.5 fusion.172
  18.0 5.3 %collective-permute-start.5 = (f32[2,2,1,64,128]{4,3,2,1,0:T(8,128)S(1)}, f32[2,2,1,64,128]{4,3,2,1,0:T(8,128)S(1)}, u32[]{:S(2)}, u32[]{:S(2)}) collective-permute-start(f32[2,2,1,64,128]{4,3,2,1,0:T(8,128)S(1)} %convolution_bitcast_fusion.42), channel_id=1, source_target_pairs={{0,1},{1,2},{2,3},{4,5},{5,6},{6,7},{8,9},{9,10},{10,11},{12,13},{... | collective-permute-start | bytes 393224 | tf_op jit(solution)/shard_map/ppermute | solution.py:16
  24.2 2.6 %collective-permute-done.5 = f32[2,2,1,64,128]{4,3,2,1,0:T(8,128)S(1)} collective-permute-done((f32[2,2,1,64,128]{4,3,2,1,0:T(8,128)S(1)}, f32[2,2,1,64,128]{4,3,2,1,0:T(8,128)S(1)}, u32[]{:S(2)}, u32[]{:S(2)}) %collective-permute-start.5) | collective-permute-done | bytes 131104 | tf_op jit(solution)/shard_map/ppermute | solution.py:16
  27.0 0.5 fusion.173
  28.7 0.4 fusion.11
  29.4 1.3 %collective-permute-start.6 = (bf16[1,2,4,64,128]{4,3,2,1,0:T(8,128)(2,1)S(1)}, bf16[1,2,4,64,128]{4,3,2,1,0:T(8,128)(2,1)S(1)}, u32[]{:S(2)}, u32[]{:S(2)}) collective-permute-start(bf16[1,2,4,64,128]{4,3,2,1,0:T(8,128)(2,1)S(1)} %slice.2391), channel_id=1, source_target_pairs={{8,0},{16,8},{24,16},{9,1},{17,9},{25,17},{10,2},{18,10},{26,18},{... | collective-permute-start | bytes 393224 | tf_op jit(solution)/shard_map/ppermute | solution.py:16
  30.9 3.0 %collective-permute-start.7 = (f32[1,2,4,64,128]{4,3,2,1,0:T(8,128)S(1)}, f32[1,2,4,64,128]{4,3,2,1,0:T(8,128)S(1)}, u32[]{:S(2)}, u32[]{:S(2)}) collective-permute-start(f32[1,2,4,64,128]{4,3,2,1,0:T(8,128)S(1)} %convolution_bitcast_fusion.32), channel_id=1, source_target_pairs={{0,8},{8,16},{16,24},{1,9},{9,17},{17,25},{2,10},{10,18},{18,26},{... | collective-permute-start | bytes 786440 | tf_op jit(solution)/shard_map/ppermute | solution.py:16
  34.1 1.3 %collective-permute-start.8 = (bf16[2,1,4,64,128]{4,3,2,1,0:T(8,128)(2,1)S(1)}, bf16[2,1,4,64,128]{4,3,2,1,0:T(8,128)(2,1)S(1)}, u32[]{:S(2)}, u32[]{:S(2)}) collective-permute-start(bf16[2,1,4,64,128]{4,3,2,1,0:T(8,128)(2,1)S(1)} %slice.2395), channel_id=1, source_target_pairs={{4,0},{5,1},{6,2},{7,3},{12,8},{13,9},{14,10},{15,11},{20,16},{21,... | collective-permute-start | bytes 393224 | tf_op jit(solution)/shard_map/ppermute | solution.py:16
  35.4 4.6 %collective-permute-start.9 = (f32[2,1,4,64,128]{4,3,2,1,0:T(8,128)S(1)}, f32[2,1,4,64,128]{4,3,2,1,0:T(8,128)S(1)}, u32[]{:S(2)}, u32[]{:S(2)}) collective-permute-start(f32[2,1,4,64,128]{4,3,2,1,0:T(8,128)S(1)} %convolution_bitcast_fusion.30), channel_id=1, source_target_pairs={{0,4},{1,5},{2,6},{3,7},{8,12},{9,13},{10,14},{11,15},{16,20},{17,... | collective-permute-start | bytes 786440 | tf_op jit(solution)/shard_map/ppermute | solution.py:16
  40.0 1.3 %collective-permute-start.10 = (bf16[2,2,1,64,128]{4,3,2,1,0:T(8,128)(2,1)S(1)}, bf16[2,2,1,64,128]{4,3,2,1,0:T(8,128)(2,1)S(1)}, u32[]{:S(2)}, u32[]{:S(2)}) collective-permute-start(bf16[2,2,1,64,128]{4,3,2,1,0:T(8,128)(2,1)S(1)} %slice.2403), channel_id=1, source_target_pairs={{1,0},{2,1},{3,2},{5,4},{6,5},{7,6},{9,8},{10,9},{11,10},{13,12},{... | collective-permute-start | bytes 196616 | tf_op jit(solution)/shard_map/ppermute | solution.py:16
  41.3 5.0 %collective-permute-start.11 = (f32[2,2,1,64,128]{4,3,2,1,0:T(8,128)S(1)}, f32[2,2,1,64,128]{4,3,2,1,0:T(8,128)S(1)}, u32[]{:S(2)}, u32[]{:S(2)}) collective-permute-start(f32[2,2,1,64,128]{4,3,2,1,0:T(8,128)S(1)} %convolution_bitcast_fusion.49), channel_id=1, source_target_pairs={{0,1},{1,2},{2,3},{4,5},{5,6},{6,7},{8,9},{9,10},{10,11},{12,13},{... | collective-permute-start | bytes 393224 | tf_op jit(solution)/shard_map/ppermute | solution.py:16
  47.3 2.4 %collective-permute-done.11 = f32[2,2,1,64,128]{4,3,2,1,0:T(8,128)S(1)} collective-permute-done((f32[2,2,1,64,128]{4,3,2,1,0:T(8,128)S(1)}, f32[2,2,1,64,128]{4,3,2,1,0:T(8,128)S(1)}, u32[]{:S(2)}, u32[]{:S(2)}) %collective-permute-start.11) | collective-permute-done | bytes 131104 | tf_op jit(solution)/shard_map/ppermute | solution.py:16
  49.9 0.4 fusion.174
  51.6 0.4 fusion.9
  52.3 1.3 %collective-permute-start.12 = (bf16[1,2,4,64,128]{4,3,2,1,0:T(8,128)(2,1)S(1)}, bf16[1,2,4,64,128]{4,3,2,1,0:T(8,128)(2,1)S(1)}, u32[]{:S(2)}, u32[]{:S(2)}) collective-permute-start(bf16[1,2,4,64,128]{4,3,2,1,0:T(8,128)(2,1)S(1)} %slice.2409), channel_id=1, source_target_pairs={{8,0},{16,8},{24,16},{9,1},{17,9},{25,17},{10,2},{18,10},{26,18},{... | collective-permute-start | bytes 393224 | tf_op jit(solution)/shard_map/ppermute | solution.py:16
  53.8 3.0 %collective-permute-start.13 = (f32[1,2,4,64,128]{4,3,2,1,0:T(8,128)S(1)}, f32[1,2,4,64,128]{4,3,2,1,0:T(8,128)S(1)}, u32[]{:S(2)}, u32[]{:S(2)}) collective-permute-start(f32[1,2,4,64,128]{4,3,2,1,0:T(8,128)S(1)} %convolution_bitcast_fusion.24), channel_id=1, source_target_pairs={{0,8},{8,16},{16,24},{1,9},{9,17},{17,25},{2,10},{10,18},{18,26},{... | collective-permute-start | bytes 786440 | tf_op jit(solution)/shard_map/ppermute | solution.py:16
  57.0 1.3 %collective-permute-start.14 = (bf16[2,1,4,64,128]{4,3,2,1,0:T(8,128)(2,1)S(1)}, bf16[2,1,4,64,128]{4,3,2,1,0:T(8,128)(2,1)S(1)}, u32[]{:S(2)}, u32[]{:S(2)}) collective-permute-start(bf16[2,1,4,64,128]{4,3,2,1,0:T(8,128)(2,1)S(1)} %slice.2413), channel_id=1, source_target_pairs={{4,0},{5,1},{6,2},{7,3},{12,8},{13,9},{14,10},{15,11},{20,16},{21,... | collective-permute-start | bytes 393224 | tf_op jit(solution)/shard_map/ppermute | solution.py:16
  58.3 4.6 %collective-permute-start.15 = (f32[2,1,4,64,128]{4,3,2,1,0:T(8,128)S(1)}, f32[2,1,4,64,128]{4,3,2,1,0:T(8,128)S(1)}, u32[]{:S(2)}, u32[]{:S(2)}) collective-permute-start(f32[2,1,4,64,128]{4,3,2,1,0:T(8,128)S(1)} %convolution_bitcast_fusion.22), channel_id=1, source_target_pairs={{0,4},{1,5},{2,6},{3,7},{8,12},{9,13},{10,14},{11,15},{16,20},{17,... | collective-permute-start | bytes 786440 | tf_op jit(solution)/shard_map/ppermute | solution.py:16
  62.9 1.3 %collective-permute-start.16 = (bf16[2,2,1,64,128]{4,3,2,1,0:T(8,128)(2,1)S(1)}, bf16[2,2,1,64,128]{4,3,2,1,0:T(8,128)(2,1)S(1)}, u32[]{:S(2)}, u32[]{:S(2)}) collective-permute-start(bf16[2,2,1,64,128]{4,3,2,1,0:T(8,128)(2,1)S(1)} %slice.2421), channel_id=1, source_target_pairs={{1,0},{2,1},{3,2},{5,4},{6,5},{7,6},{9,8},{10,9},{11,10},{13,12},{... | collective-permute-start | bytes 196616 | tf_op jit(solution)/shard_map/ppermute | solution.py:16
  64.2 5.0 %collective-permute-start.17 = (f32[2,2,1,64,128]{4,3,2,1,0:T(8,128)S(1)}, f32[2,2,1,64,128]{4,3,2,1,0:T(8,128)S(1)}, u32[]{:S(2)}, u32[]{:S(2)}) collective-permute-start(f32[2,2,1,64,128]{4,3,2,1,0:T(8,128)S(1)} %convolution_bitcast_fusion.47), channel_id=1, source_target_pairs={{0,1},{1,2},{2,3},{4,5},{5,6},{6,7},{8,9},{9,10},{10,11},{12,13},{... | collective-permute-start | bytes 393224 | tf_op jit(solution)/shard_map/ppermute | solution.py:16
  70.2 2.3 %collective-permute-done.17 = f32[2,2,1,64,128]{4,3,2,1,0:T(8,128)S(1)} collective-permute-done((f32[2,2,1,64,128]{4,3,2,1,0:T(8,128)S(1)}, f32[2,2,1,64,128]{4,3,2,1,0:T(8,128)S(1)}, u32[]{:S(2)}, u32[]{:S(2)}) %collective-permute-start.17) | collective-permute-done | bytes 131104 | tf_op jit(solution)/shard_map/ppermute | solution.py:16
  72.7 0.4 fusion.175
  74.4 0.4 fusion.7
  75.1 1.3 %collective-permute-start.18 = (bf16[1,2,4,64,128]{4,3,2,1,0:T(8,128)(2,1)S(1)}, bf16[1,2,4,64,128]{4,3,2,1,0:T(8,128)(2,1)S(1)}, u32[]{:S(2)}, u32[]{:S(2)}) collective-permute-start(bf16[1,2,4,64,128]{4,3,2,1,0:T(8,128)(2,1)S(1)} %slice.2427), channel_id=1, source_target_pairs={{8,0},{16,8},{24,16},{9,1},{17,9},{25,17},{10,2},{18,10},{26,18},{... | collective-permute-start | bytes 393224 | tf_op jit(solution)/shard_map/ppermute | solution.py:16
  76.6 3.0 %collective-permute-start.19 = (f32[1,2,4,64,128]{4,3,2,1,0:T(8,128)S(1)}, f32[1,2,4,64,128]{4,3,2,1,0:T(8,128)S(1)}, u32[]{:S(2)}, u32[]{:S(2)}) collective-permute-start(f32[1,2,4,64,128]{4,3,2,1,0:T(8,128)S(1)} %convolution_bitcast_fusion.16), channel_id=1, source_target_pairs={{0,8},{8,16},{16,24},{1,9},{9,17},{17,25},{2,10},{10,18},{18,26},{... | collective-permute-start | bytes 786440 | tf_op jit(solution)/shard_map/ppermute | solution.py:16
  79.8 1.3 %collective-permute-start.20 = (bf16[2,1,4,64,128]{4,3,2,1,0:T(8,128)(2,1)S(1)}, bf16[2,1,4,64,128]{4,3,2,1,0:T(8,128)(2,1)S(1)}, u32[]{:S(2)}, u32[]{:S(2)}) collective-permute-start(bf16[2,1,4,64,128]{4,3,2,1,0:T(8,128)(2,1)S(1)} %slice.2431), channel_id=1, source_target_pairs={{4,0},{5,1},{6,2},{7,3},{12,8},{13,9},{14,10},{15,11},{20,16},{21,... | collective-permute-start | bytes 393224 | tf_op jit(solution)/shard_map/ppermute | solution.py:16
  81.1 4.6 %collective-permute-start.21 = (f32[2,1,4,64,128]{4,3,2,1,0:T(8,128)S(1)}, f32[2,1,4,64,128]{4,3,2,1,0:T(8,128)S(1)}, u32[]{:S(2)}, u32[]{:S(2)}) collective-permute-start(f32[2,1,4,64,128]{4,3,2,1,0:T(8,128)S(1)} %convolution_bitcast_fusion.14), channel_id=1, source_target_pairs={{0,4},{1,5},{2,6},{3,7},{8,12},{9,13},{10,14},{11,15},{16,20},{17,... | collective-permute-start | bytes 786440 | tf_op jit(solution)/shard_map/ppermute | solution.py:16
  85.7 1.3 %collective-permute-start.22 = (bf16[2,2,1,64,128]{4,3,2,1,0:T(8,128)(2,1)S(1)}, bf16[2,2,1,64,128]{4,3,2,1,0:T(8,128)(2,1)S(1)}, u32[]{:S(2)}, u32[]{:S(2)}) collective-permute-start(bf16[2,2,1,64,128]{4,3,2,1,0:T(8,128)(2,1)S(1)} %slice.2439), channel_id=1, source_target_pairs={{1,0},{2,1},{3,2},{5,4},{6,5},{7,6},{9,8},{10,9},{11,10},{13,12},{... | collective-permute-start | bytes 196616 | tf_op jit(solution)/shard_map/ppermute | solution.py:16
  87.0 5.0 %collective-permute-start.23 = (f32[2,2,1,64,128]{4,3,2,1,0:T(8,128)S(1)}, f32[2,2,1,64,128]{4,3,2,1,0:T(8,128)S(1)}, u32[]{:S(2)}, u32[]{:S(2)}) collective-permute-start(f32[2,2,1,64,128]{4,3,2,1,0:T(8,128)S(1)} %convolution_bitcast_fusion.45), channel_id=1, source_target_pairs={{0,1},{1,2},{2,3},{4,5},{5,6},{6,7},{8,9},{9,10},{10,11},{12,13},{... | collective-permute-start | bytes 393224 | tf_op jit(solution)/shard_map/ppermute | solution.py:16
  93.0 2.2 %collective-permute-done.23 = f32[2,2,1,64,128]{4,3,2,1,0:T(8,128)S(1)} collective-permute-done((f32[2,2,1,64,128]{4,3,2,1,0:T(8,128)S(1)}, f32[2,2,1,64,128]{4,3,2,1,0:T(8,128)S(1)}, u32[]{:S(2)}, u32[]{:S(2)}) %collective-permute-start.23) | collective-permute-done | bytes 131104 | tf_op jit(solution)/shard_map/ppermute | solution.py:16
  95.4 0.5 fusion.176
  97.1 0.4 fusion.5
  97.8 1.3 %collective-permute-start.24 = (bf16[1,2,4,64,128]{4,3,2,1,0:T(8,128)(2,1)S(1)}, bf16[1,2,4,64,128]{4,3,2,1,0:T(8,128)(2,1)S(1)}, u32[]{:S(2)}, u32[]{:S(2)}) collective-permute-start(bf16[1,2,4,64,128]{4,3,2,1,0:T(8,128)(2,1)S(1)} %slice.2445), channel_id=1, source_target_pairs={{8,0},{16,8},{24,16},{9,1},{17,9},{25,17},{10,2},{18,10},{26,18},{... | collective-permute-start | bytes 393224 | tf_op jit(solution)/shard_map/ppermute | solution.py:16
  99.3 3.0 %collective-permute-start.25 = (f32[1,2,4,64,128]{4,3,2,1,0:T(8,128)S(1)}, f32[1,2,4,64,128]{4,3,2,1,0:T(8,128)S(1)}, u32[]{:S(2)}, u32[]{:S(2)}) collective-permute-start(f32[1,2,4,64,128]{4,3,2,1,0:T(8,128)S(1)} %convolution_bitcast_fusion.8), channel_id=1, source_target_pairs={{0,8},{8,16},{16,24},{1,9},{9,17},{17,25},{2,10},{10,18},{18,26},{... | collective-permute-start | bytes 786440 | tf_op jit(solution)/shard_map/ppermute | solution.py:16
  102.5 1.3 %collective-permute-start.26 = (bf16[2,1,4,64,128]{4,3,2,1,0:T(8,128)(2,1)S(1)}, bf16[2,1,4,64,128]{4,3,2,1,0:T(8,128)(2,1)S(1)}, u32[]{:S(2)}, u32[]{:S(2)}) collective-permute-start(bf16[2,1,4,64,128]{4,3,2,1,0:T(8,128)(2,1)S(1)} %slice.2449), channel_id=1, source_target_pairs={{4,0},{5,1},{6,2},{7,3},{12,8},{13,9},{14,10},{15,11},{20,16},{21,... | collective-permute-start | bytes 393224 | tf_op jit(solution)/shard_map/ppermute | solution.py:16
  103.8 4.6 %collective-permute-start.27 = (f32[2,1,4,64,128]{4,3,2,1,0:T(8,128)S(1)}, f32[2,1,4,64,128]{4,3,2,1,0:T(8,128)S(1)}, u32[]{:S(2)}, u32[]{:S(2)}) collective-permute-start(f32[2,1,4,64,128]{4,3,2,1,0:T(8,128)S(1)} %convolution_bitcast_fusion.6), channel_id=1, source_target_pairs={{0,4},{1,5},{2,6},{3,7},{8,12},{9,13},{10,14},{11,15},{16,20},{17,... | collective-permute-start | bytes 786440 | tf_op jit(solution)/shard_map/ppermute | solution.py:16
  108.4 1.3 %collective-permute-start.28 = (bf16[2,2,1,64,128]{4,3,2,1,0:T(8,128)(2,1)S(1)}, bf16[2,2,1,64,128]{4,3,2,1,0:T(8,128)(2,1)S(1)}, u32[]{:S(2)}, u32[]{:S(2)}) collective-permute-start(bf16[2,2,1,64,128]{4,3,2,1,0:T(8,128)(2,1)S(1)} %slice.2457), channel_id=1, source_target_pairs={{1,0},{2,1},{3,2},{5,4},{6,5},{7,6},{9,8},{10,9},{11,10},{13,12},{... | collective-permute-start | bytes 196616 | tf_op jit(solution)/shard_map/ppermute | solution.py:16
  109.7 5.0 %collective-permute-start.29 = (f32[2,2,1,64,128]{4,3,2,1,0:T(8,128)S(1)}, f32[2,2,1,64,128]{4,3,2,1,0:T(8,128)S(1)}, u32[]{:S(2)}, u32[]{:S(2)}) collective-permute-start(f32[2,2,1,64,128]{4,3,2,1,0:T(8,128)S(1)} %convolution_bitcast_fusion.43), channel_id=1, source_target_pairs={{0,1},{1,2},{2,3},{4,5},{5,6},{6,7},{8,9},{9,10},{10,11},{12,13},{... | collective-permute-start | bytes 393224 | tf_op jit(solution)/shard_map/ppermute | solution.py:16
  115.7 2.1 %collective-permute-done.29 = f32[2,2,1,64,128]{4,3,2,1,0:T(8,128)S(1)} collective-permute-done((f32[2,2,1,64,128]{4,3,2,1,0:T(8,128)S(1)}, f32[2,2,1,64,128]{4,3,2,1,0:T(8,128)S(1)}, u32[]{:S(2)}, u32[]{:S(2)}) %collective-permute-start.29) | collective-permute-done | bytes 131104 | tf_op jit(solution)/shard_map/ppermute | solution.py:16
  117.8 0.9 convert_subtract_fusion
  (119 shorter events, 14.9 us)
Async XLA Ops:
  0.0 15.7 %copy-start = (bf16[2,2,4,128,128]{4,3,2,1,0:T(8,128)(2,1)S(1)}, bf16[2,2,4,128,128]{4,3,2,1,0:T(8,128)(2,1)}, u32[]{:S(2)}) copy-start(bf16[2,2,4,128,128]{4,3,2,1,0:T(8,128)(2,1)} %param.125) | copy-start | bytes 1572868
  1.0 17.0 %collective-permute-start = (bf16[1,2,4,64,128]{4,3,2,1,0:T(8,128)(2,1)S(1)}, bf16[1,2,4,64,128]{4,3,2,1,0:T(8,128)(2,1)S(1)}, u32[]{:S(2)}, u32[]{:S(2)}) collective-permute-start(bf16[1,2,4,64,128]{4,3,2,1,0:T(8,128)(2,1)S(1)} %slice.2264), channel_id=1, source_target_pairs={{8,0},{16,8},{24,16},{9,1},{17,9},{25,17},{10,2},{18,10},{26,18},{... | collective-permute-start | bytes 393224 | tf_op jit(solution)/shard_map/ppermute | solution.py:16
  3.0 1.6 %copy-start.1 = (bf16[2,2,4,64,128]{4,3,2,1,0:T(8,128)(2,1)S(1)}, bf16[2,2,4,64,128]{4,3,2,1,0:T(8,128)(2,1)}, u32[]{:S(2)}) copy-start(bf16[2,2,4,64,128]{4,3,2,1,0:T(8,128)(2,1)} %param.124) | copy-start | bytes 786436
  4.8 18.7 %collective-permute-start.1 = (f32[1,2,4,64,128]{4,3,2,1,0:T(8,128)S(1)}, f32[1,2,4,64,128]{4,3,2,1,0:T(8,128)S(1)}, u32[]{:S(2)}, u32[]{:S(2)}) collective-permute-start(f32[1,2,4,64,128]{4,3,2,1,0:T(8,128)S(1)} %convolution_bitcast_fusion.3), channel_id=1, source_target_pairs={{0,8},{8,16},{16,24},{1,9},{9,17},{17,25},{2,10},{10,18},{18,26},{... | collective-permute-start | bytes 786440 | tf_op jit(solution)/shard_map/ppermute | solution.py:16
  7.9 15.7 %collective-permute-start.2 = (bf16[2,1,4,64,128]{4,3,2,0,1:T(8,128)(2,1)S(1)}, bf16[2,1,4,64,128]{4,3,2,0,1:T(8,128)(2,1)S(1)}, u32[]{:S(2)}, u32[]{:S(2)}) collective-permute-start(bf16[2,1,4,64,128]{4,3,2,0,1:T(8,128)(2,1)S(1)} %slice_bitcast_fusion.31), channel_id=1, source_target_pairs={{4,0},{5,1},{6,2},{7,3},{12,8},{13,9},{14,10},{15,11},{20,16},{21,... | collective-permute-start | bytes 393224 | tf_op jit(solution)/shard_map/ppermute | solution.py:16
  9.5 14.4 %collective-permute-start.3 = (f32[2,1,4,64,128]{4,3,2,1,0:T(8,128)S(1)}, f32[2,1,4,64,128]{4,3,2,1,0:T(8,128)S(1)}, u32[]{:S(2)}, u32[]{:S(2)}) collective-permute-start(f32[2,1,4,64,128]{4,3,2,1,0:T(8,128)S(1)} %convolution_bitcast_fusion.2), channel_id=1, source_target_pairs={{0,4},{1,5},{2,6},{3,7},{8,12},{9,13},{10,14},{11,15},{16,20},{17,... | collective-permute-start | bytes 786440 | tf_op jit(solution)/shard_map/ppermute | solution.py:16
  14.3 9.6 %collective-permute-start.4 = (bf16[2,2,1,64,128]{4,3,1,0,2:T(8,128)(2,1)S(1)}, bf16[2,2,1,64,128]{4,3,1,0,2:T(8,128)(2,1)S(1)}, u32[]{:S(2)}, u32[]{:S(2)}) collective-permute-start(bf16[2,2,1,64,128]{4,3,1,0,2:T(8,128)(2,1)S(1)} %slice_bitcast_fusion.40), channel_id=1, source_target_pairs={{1,0},{2,1},{3,2},{5,4},{6,5},{7,6},{9,8},{10,9},{11,10},{13,12},{... | collective-permute-start | bytes 196616 | tf_op jit(solution)/shard_map/ppermute | solution.py:16
  18.0 8.9 %collective-permute-start.5 = (f32[2,2,1,64,128]{4,3,2,1,0:T(8,128)S(1)}, f32[2,2,1,64,128]{4,3,2,1,0:T(8,128)S(1)}, u32[]{:S(2)}, u32[]{:S(2)}) collective-permute-start(f32[2,2,1,64,128]{4,3,2,1,0:T(8,128)S(1)} %convolution_bitcast_fusion.42), channel_id=1, source_target_pairs={{0,1},{1,2},{2,3},{4,5},{5,6},{6,7},{8,9},{9,10},{10,11},{12,13},{... | collective-permute-start | bytes 393224 | tf_op jit(solution)/shard_map/ppermute | solution.py:16
  29.4 11.9 %collective-permute-start.6 = (bf16[1,2,4,64,128]{4,3,2,1,0:T(8,128)(2,1)S(1)}, bf16[1,2,4,64,128]{4,3,2,1,0:T(8,128)(2,1)S(1)}, u32[]{:S(2)}, u32[]{:S(2)}) collective-permute-start(bf16[1,2,4,64,128]{4,3,2,1,0:T(8,128)(2,1)S(1)} %slice.2391), channel_id=1, source_target_pairs={{8,0},{16,8},{24,16},{9,1},{17,9},{25,17},{10,2},{18,10},{26,18},{... | collective-permute-start | bytes 393224 | tf_op jit(solution)/shard_map/ppermute | solution.py:16
  30.9 15.8 %collective-permute-start.7 = (f32[1,2,4,64,128]{4,3,2,1,0:T(8,128)S(1)}, f32[1,2,4,64,128]{4,3,2,1,0:T(8,128)S(1)}, u32[]{:S(2)}, u32[]{:S(2)}) collective-permute-start(f32[1,2,4,64,128]{4,3,2,1,0:T(8,128)S(1)} %convolution_bitcast_fusion.32), channel_id=1, source_target_pairs={{0,8},{8,16},{16,24},{1,9},{9,17},{17,25},{2,10},{10,18},{18,26},{... | collective-permute-start | bytes 786440 | tf_op jit(solution)/shard_map/ppermute | solution.py:16
  34.1 12.6 %collective-permute-start.8 = (bf16[2,1,4,64,128]{4,3,2,1,0:T(8,128)(2,1)S(1)}, bf16[2,1,4,64,128]{4,3,2,1,0:T(8,128)(2,1)S(1)}, u32[]{:S(2)}, u32[]{:S(2)}) collective-permute-start(bf16[2,1,4,64,128]{4,3,2,1,0:T(8,128)(2,1)S(1)} %slice.2395), channel_id=1, source_target_pairs={{4,0},{5,1},{6,2},{7,3},{12,8},{13,9},{14,10},{15,11},{20,16},{21,... | collective-permute-start | bytes 393224 | tf_op jit(solution)/shard_map/ppermute | solution.py:16
  35.4 11.6 %collective-permute-start.9 = (f32[2,1,4,64,128]{4,3,2,1,0:T(8,128)S(1)}, f32[2,1,4,64,128]{4,3,2,1,0:T(8,128)S(1)}, u32[]{:S(2)}, u32[]{:S(2)}) collective-permute-start(f32[2,1,4,64,128]{4,3,2,1,0:T(8,128)S(1)} %convolution_bitcast_fusion.30), channel_id=1, source_target_pairs={{0,4},{1,5},{2,6},{3,7},{8,12},{9,13},{10,14},{11,15},{16,20},{17,... | collective-permute-start | bytes 786440 | tf_op jit(solution)/shard_map/ppermute | solution.py:16
  40.0 7.2 %collective-permute-start.10 = (bf16[2,2,1,64,128]{4,3,2,1,0:T(8,128)(2,1)S(1)}, bf16[2,2,1,64,128]{4,3,2,1,0:T(8,128)(2,1)S(1)}, u32[]{:S(2)}, u32[]{:S(2)}) collective-permute-start(bf16[2,2,1,64,128]{4,3,2,1,0:T(8,128)(2,1)S(1)} %slice.2403), channel_id=1, source_target_pairs={{1,0},{2,1},{3,2},{5,4},{6,5},{7,6},{9,8},{10,9},{11,10},{13,12},{... | collective-permute-start | bytes 196616 | tf_op jit(solution)/shard_map/ppermute | solution.py:16
  41.3 8.4 %collective-permute-start.11 = (f32[2,2,1,64,128]{4,3,2,1,0:T(8,128)S(1)}, f32[2,2,1,64,128]{4,3,2,1,0:T(8,128)S(1)}, u32[]{:S(2)}, u32[]{:S(2)}) collective-permute-start(f32[2,2,1,64,128]{4,3,2,1,0:T(8,128)S(1)} %convolution_bitcast_fusion.49), channel_id=1, source_target_pairs={{0,1},{1,2},{2,3},{4,5},{5,6},{6,7},{8,9},{9,10},{10,11},{12,13},{... | collective-permute-start | bytes 393224 | tf_op jit(solution)/shard_map/ppermute | solution.py:16
  52.3 11.9 %collective-permute-start.12 = (bf16[1,2,4,64,128]{4,3,2,1,0:T(8,128)(2,1)S(1)}, bf16[1,2,4,64,128]{4,3,2,1,0:T(8,128)(2,1)S(1)}, u32[]{:S(2)}, u32[]{:S(2)}) collective-permute-start(bf16[1,2,4,64,128]{4,3,2,1,0:T(8,128)(2,1)S(1)} %slice.2409), channel_id=1, source_target_pairs={{8,0},{16,8},{24,16},{9,1},{17,9},{25,17},{10,2},{18,10},{26,18},{... | collective-permute-start | bytes 393224 | tf_op jit(solution)/shard_map/ppermute | solution.py:16
  53.8 15.8 %collective-permute-start.13 = (f32[1,2,4,64,128]{4,3,2,1,0:T(8,128)S(1)}, f32[1,2,4,64,128]{4,3,2,1,0:T(8,128)S(1)}, u32[]{:S(2)}, u32[]{:S(2)}) collective-permute-start(f32[1,2,4,64,128]{4,3,2,1,0:T(8,128)S(1)} %convolution_bitcast_fusion.24), channel_id=1, source_target_pairs={{0,8},{8,16},{16,24},{1,9},{9,17},{17,25},{2,10},{10,18},{18,26},{... | collective-permute-start | bytes 786440 | tf_op jit(solution)/shard_map/ppermute | solution.py:16
  57.0 12.6 %collective-permute-start.14 = (bf16[2,1,4,64,128]{4,3,2,1,0:T(8,128)(2,1)S(1)}, bf16[2,1,4,64,128]{4,3,2,1,0:T(8,128)(2,1)S(1)}, u32[]{:S(2)}, u32[]{:S(2)}) collective-permute-start(bf16[2,1,4,64,128]{4,3,2,1,0:T(8,128)(2,1)S(1)} %slice.2413), channel_id=1, source_target_pairs={{4,0},{5,1},{6,2},{7,3},{12,8},{13,9},{14,10},{15,11},{20,16},{21,... | collective-permute-start | bytes 393224 | tf_op jit(solution)/shard_map/ppermute | solution.py:16
  58.3 11.6 %collective-permute-start.15 = (f32[2,1,4,64,128]{4,3,2,1,0:T(8,128)S(1)}, f32[2,1,4,64,128]{4,3,2,1,0:T(8,128)S(1)}, u32[]{:S(2)}, u32[]{:S(2)}) collective-permute-start(f32[2,1,4,64,128]{4,3,2,1,0:T(8,128)S(1)} %convolution_bitcast_fusion.22), channel_id=1, source_target_pairs={{0,4},{1,5},{2,6},{3,7},{8,12},{9,13},{10,14},{11,15},{16,20},{17,... | collective-permute-start | bytes 786440 | tf_op jit(solution)/shard_map/ppermute | solution.py:16
  62.9 7.1 %collective-permute-start.16 = (bf16[2,2,1,64,128]{4,3,2,1,0:T(8,128)(2,1)S(1)}, bf16[2,2,1,64,128]{4,3,2,1,0:T(8,128)(2,1)S(1)}, u32[]{:S(2)}, u32[]{:S(2)}) collective-permute-start(bf16[2,2,1,64,128]{4,3,2,1,0:T(8,128)(2,1)S(1)} %slice.2421), channel_id=1, source_target_pairs={{1,0},{2,1},{3,2},{5,4},{6,5},{7,6},{9,8},{10,9},{11,10},{13,12},{... | collective-permute-start | bytes 196616 | tf_op jit(solution)/shard_map/ppermute | solution.py:16
  64.2 8.4 %collective-permute-start.17 = (f32[2,2,1,64,128]{4,3,2,1,0:T(8,128)S(1)}, f32[2,2,1,64,128]{4,3,2,1,0:T(8,128)S(1)}, u32[]{:S(2)}, u32[]{:S(2)}) collective-permute-start(f32[2,2,1,64,128]{4,3,2,1,0:T(8,128)S(1)} %convolution_bitcast_fusion.47), channel_id=1, source_target_pairs={{0,1},{1,2},{2,3},{4,5},{5,6},{6,7},{8,9},{9,10},{10,11},{12,13},{... | collective-permute-start | bytes 393224 | tf_op jit(solution)/shard_map/ppermute | solution.py:16
  75.1 11.9 %collective-permute-start.18 = (bf16[1,2,4,64,128]{4,3,2,1,0:T(8,128)(2,1)S(1)}, bf16[1,2,4,64,128]{4,3,2,1,0:T(8,128)(2,1)S(1)}, u32[]{:S(2)}, u32[]{:S(2)}) collective-permute-start(bf16[1,2,4,64,128]{4,3,2,1,0:T(8,128)(2,1)S(1)} %slice.2427), channel_id=1, source_target_pairs={{8,0},{16,8},{24,16},{9,1},{17,9},{25,17},{10,2},{18,10},{26,18},{... | collective-permute-start | bytes 393224 | tf_op jit(solution)/shard_map/ppermute | solution.py:16
  76.6 15.8 %collective-permute-start.19 = (f32[1,2,4,64,128]{4,3,2,1,0:T(8,128)S(1)}, f32[1,2,4,64,128]{4,3,2,1,0:T(8,128)S(1)}, u32[]{:S(2)}, u32[]{:S(2)}) collective-permute-start(f32[1,2,4,64,128]{4,3,2,1,0:T(8,128)S(1)} %convolution_bitcast_fusion.16), channel_id=1, source_target_pairs={{0,8},{8,16},{16,24},{1,9},{9,17},{17,25},{2,10},{10,18},{18,26},{... | collective-permute-start | bytes 786440 | tf_op jit(solution)/shard_map/ppermute | solution.py:16
  79.8 12.6 %collective-permute-start.20 = (bf16[2,1,4,64,128]{4,3,2,1,0:T(8,128)(2,1)S(1)}, bf16[2,1,4,64,128]{4,3,2,1,0:T(8,128)(2,1)S(1)}, u32[]{:S(2)}, u32[]{:S(2)}) collective-permute-start(bf16[2,1,4,64,128]{4,3,2,1,0:T(8,128)(2,1)S(1)} %slice.2431), channel_id=1, source_target_pairs={{4,0},{5,1},{6,2},{7,3},{12,8},{13,9},{14,10},{15,11},{20,16},{21,... | collective-permute-start | bytes 393224 | tf_op jit(solution)/shard_map/ppermute | solution.py:16
  81.1 11.6 %collective-permute-start.21 = (f32[2,1,4,64,128]{4,3,2,1,0:T(8,128)S(1)}, f32[2,1,4,64,128]{4,3,2,1,0:T(8,128)S(1)}, u32[]{:S(2)}, u32[]{:S(2)}) collective-permute-start(f32[2,1,4,64,128]{4,3,2,1,0:T(8,128)S(1)} %convolution_bitcast_fusion.14), channel_id=1, source_target_pairs={{0,4},{1,5},{2,6},{3,7},{8,12},{9,13},{10,14},{11,15},{16,20},{17,... | collective-permute-start | bytes 786440 | tf_op jit(solution)/shard_map/ppermute | solution.py:16
  85.7 7.1 %collective-permute-start.22 = (bf16[2,2,1,64,128]{4,3,2,1,0:T(8,128)(2,1)S(1)}, bf16[2,2,1,64,128]{4,3,2,1,0:T(8,128)(2,1)S(1)}, u32[]{:S(2)}, u32[]{:S(2)}) collective-permute-start(bf16[2,2,1,64,128]{4,3,2,1,0:T(8,128)(2,1)S(1)} %slice.2439), channel_id=1, source_target_pairs={{1,0},{2,1},{3,2},{5,4},{6,5},{7,6},{9,8},{10,9},{11,10},{13,12},{... | collective-permute-start | bytes 196616 | tf_op jit(solution)/shard_map/ppermute | solution.py:16
  87.0 8.2 %collective-permute-start.23 = (f32[2,2,1,64,128]{4,3,2,1,0:T(8,128)S(1)}, f32[2,2,1,64,128]{4,3,2,1,0:T(8,128)S(1)}, u32[]{:S(2)}, u32[]{:S(2)}) collective-permute-start(f32[2,2,1,64,128]{4,3,2,1,0:T(8,128)S(1)} %convolution_bitcast_fusion.45), channel_id=1, source_target_pairs={{0,1},{1,2},{2,3},{4,5},{5,6},{6,7},{8,9},{9,10},{10,11},{12,13},{... | collective-permute-start | bytes 393224 | tf_op jit(solution)/shard_map/ppermute | solution.py:16
  97.8 11.9 %collective-permute-start.24 = (bf16[1,2,4,64,128]{4,3,2,1,0:T(8,128)(2,1)S(1)}, bf16[1,2,4,64,128]{4,3,2,1,0:T(8,128)(2,1)S(1)}, u32[]{:S(2)}, u32[]{:S(2)}) collective-permute-start(bf16[1,2,4,64,128]{4,3,2,1,0:T(8,128)(2,1)S(1)} %slice.2445), channel_id=1, source_target_pairs={{8,0},{16,8},{24,16},{9,1},{17,9},{25,17},{10,2},{18,10},{26,18},{... | collective-permute-start | bytes 393224 | tf_op jit(solution)/shard_map/ppermute | solution.py:16
  99.3 15.8 %collective-permute-start.25 = (f32[1,2,4,64,128]{4,3,2,1,0:T(8,128)S(1)}, f32[1,2,4,64,128]{4,3,2,1,0:T(8,128)S(1)}, u32[]{:S(2)}, u32[]{:S(2)}) collective-permute-start(f32[1,2,4,64,128]{4,3,2,1,0:T(8,128)S(1)} %convolution_bitcast_fusion.8), channel_id=1, source_target_pairs={{0,8},{8,16},{16,24},{1,9},{9,17},{17,25},{2,10},{10,18},{18,26},{... | collective-permute-start | bytes 786440 | tf_op jit(solution)/shard_map/ppermute | solution.py:16
  102.5 12.6 %collective-permute-start.26 = (bf16[2,1,4,64,128]{4,3,2,1,0:T(8,128)(2,1)S(1)}, bf16[2,1,4,64,128]{4,3,2,1,0:T(8,128)(2,1)S(1)}, u32[]{:S(2)}, u32[]{:S(2)}) collective-permute-start(bf16[2,1,4,64,128]{4,3,2,1,0:T(8,128)(2,1)S(1)} %slice.2449), channel_id=1, source_target_pairs={{4,0},{5,1},{6,2},{7,3},{12,8},{13,9},{14,10},{15,11},{20,16},{21,... | collective-permute-start | bytes 393224 | tf_op jit(solution)/shard_map/ppermute | solution.py:16
  103.8 11.6 %collective-permute-start.27 = (f32[2,1,4,64,128]{4,3,2,1,0:T(8,128)S(1)}, f32[2,1,4,64,128]{4,3,2,1,0:T(8,128)S(1)}, u32[]{:S(2)}, u32[]{:S(2)}) collective-permute-start(f32[2,1,4,64,128]{4,3,2,1,0:T(8,128)S(1)} %convolution_bitcast_fusion.6), channel_id=1, source_target_pairs={{0,4},{1,5},{2,6},{3,7},{8,12},{9,13},{10,14},{11,15},{16,20},{17,... | collective-permute-start | bytes 786440 | tf_op jit(solution)/shard_map/ppermute | solution.py:16
  108.4 7.1 %collective-permute-start.28 = (bf16[2,2,1,64,128]{4,3,2,1,0:T(8,128)(2,1)S(1)}, bf16[2,2,1,64,128]{4,3,2,1,0:T(8,128)(2,1)S(1)}, u32[]{:S(2)}, u32[]{:S(2)}) collective-permute-start(bf16[2,2,1,64,128]{4,3,2,1,0:T(8,128)(2,1)S(1)} %slice.2457), channel_id=1, source_target_pairs={{1,0},{2,1},{3,2},{5,4},{6,5},{7,6},{9,8},{10,9},{11,10},{13,12},{... | collective-permute-start | bytes 196616 | tf_op jit(solution)/shard_map/ppermute | solution.py:16
  109.7 8.1 %collective-permute-start.29 = (f32[2,2,1,64,128]{4,3,2,1,0:T(8,128)S(1)}, f32[2,2,1,64,128]{4,3,2,1,0:T(8,128)S(1)}, u32[]{:S(2)}, u32[]{:S(2)}) collective-permute-start(f32[2,2,1,64,128]{4,3,2,1,0:T(8,128)S(1)} %convolution_bitcast_fusion.43), channel_id=1, source_target_pairs={{0,1},{1,2},{2,3},{4,5},{5,6},{6,7},{8,9},{9,10},{10,11},{12,13},{... | collective-permute-start | bytes 393224 | tf_op jit(solution)/shard_map/ppermute | solution.py:16
where the time goes:
time: 120 us; the launch traced here: 119 us
  starting transfers between devices  83.1 us (69%)
  matrix products  17.1 us (14%)
  waiting for transfers between devices  11.8 us (10%)
  other arithmetic  4.45 us (4%)
  local copies, waits for them, and re-layouts  1.26 us (1%)
    ppermute x30, starting transfers between devices, passed_along(): return lax.ppermute(block, axis, route)  83.1 us
    ppermute x30, waiting for transfers between devices, passed_along(): return lax.ppermute(block, axis, route)  11.8 us
    dot_general x35, matrix products, block_apply(): jnp.einsum('...pq,...kq->...kp', blocks, vecs, preferred_element_type=jnp...  10.9 us
    dot_general x30, matrix products, block_transposed(): jnp.einsum('...pq,...kp->...kq', blocks, vecs, preferred_element_type=jnp...  6.16 us
  transfers between devices with their start and end apart: 30, of which 6 were waited for; matrix products, arithmetic and copies ran while one was open for 9% of the time, Pallas kernels for 0%

commit v1 on v0

v1 whole, which is shorter than its diff:
```python
import functools

import jax
import jax.numpy as jnp
from jax import lax
from jax.experimental import pallas as pl
from jax.experimental.pallas import tpu as pltpu
from jax.sharding import PartitionSpec as P

STEPS = 5

center_shift = 0.25
half_inverse = 0.5

BF16 = jnp.bfloat16
F32 = jnp.float32
MESH = pl.DeviceIdType.MESH
AXES = ("gx", "gy", "gz")


def apply_block(vec, block):
    return lax.dot_general(vec, block, (((1,), (1,)), ((), ())), preferred_element_type=F32)


def apply_transposed(vec, block):
    return lax.dot_general(vec, block, (((1,), (0,)), ((), ())), preferred_element_type=F32)


def kernel(sizes, bonds, trial, onsite, coupling, out, vecs, blocks, acc,
           above_x, above_y, above_z, below_x, below_y, below_z,
           part_x, part_y, part_z, send_sem, recv_sem):
    nx, ny, nz = trial.shape[:3]
    order = [0, nz - 1] + list(range(1, nz - 1)) if nz > 1 else [0]
    place = {z: i for i, z in enumerate(order)}
    chunks = [(0, min(2, nz))] + ([(2, nz)] if nz > 2 else [])

    me = [lax.axis_index(a) for a in AXES]
    has_up = [me[d] < sizes[d] - 1 for d in range(3)]
    has_down = [me[d] > 0 for d in range(3)]

    def copies(slot, chunk):
        lo, hi = chunks[chunk]
        zs = pl.ds(lo, hi - lo)
        rows = [
            (0, -1, vecs.at[slot, zs, 0], above_x.at[slot, zs]),
            (0, 1, part_x.at[slot, zs], below_x.at[slot, zs]),
            (1, -1, vecs.at[slot, zs, :, 0], above_y.at[slot, zs]),
            (1, 1, part_y.at[slot, zs], below_y.at[slot, zs]),
        ]
        if chunk == 0:
            rows += [
                (2, -1, vecs.at[slot, place[0]], above_z.at[slot]),
                (2, 1, part_z.at[slot], below_z.at[slot]),
            ]
        result = []
        for i, (d, way, src, dst) in enumerate(rows):
            copy = pltpu.make_async_remote_copy(
                src_ref=src, dst_ref=dst,
                send_sem=send_sem.at[slot, chunk, i], recv_sem=recv_sem.at[slot, chunk, i],
                device_id={AXES[d]: me[d] + way}, device_id_type=MESH)
            sends = has_up[d] if way > 0 else has_down[d]
            receives = has_down[d] if way > 0 else has_up[d]
            result.append((d, way, copy, sends, receives))
        return result

    def start(slot, chunk, way):
        for d, w, copy, sends, _ in copies(slot, chunk):
            if w == way:
                pl.when(sends)(copy.start)

    def finish(slot, chunk):
        for d, w, copy, sends, receives in copies(slot, chunk):
            pl.when(sends)(copy.wait_send)
            pl.when(receives)(copy.wait_recv)

    def cells(chunk):
        lo, hi = chunks[chunk]
        return [(i, order[i], x, y) for i in range(lo, hi) for x in range(nx) for y in range(ny)]

    def partials(slot, chunk):
        for i, z, x, y in cells(chunk):
            v = vecs[slot, i, x, y]
            if x == nx - 1:
                part_x[slot, i, y] = apply_transposed(v, blocks[0, x, y, z]).astype(BF16)
            if y == ny - 1:
                part_y[slot, i, x] = apply_transposed(v, blocks[1, x, y, z]).astype(BF16)
            if z == nz - 1:
                part_z[slot, x, y] = apply_transposed(v, blocks[2, x, y, z]).astype(BF16)

    def local_terms(slot):
        for chunk in range(len(chunks)):
            for i, z, x, y in cells(chunk):
                v = vecs[slot, i, x, y]
                total = apply_transposed(v, onsite[x, y, z])
                if x + 1 < nx:
                    total += apply_block(vecs[slot, i, x + 1, y], blocks[0, x, y, z])
                if x > 0:
                    total += apply_transposed(vecs[slot, i, x - 1, y], blocks[0, x - 1, y, z])
                if y + 1 < ny:
                    total += apply_block(vecs[slot, i, x, y + 1], blocks[1, x, y, z])
                if y > 0:
                    total += apply_transposed(vecs[slot, i, x, y - 1], blocks[1, x, y - 1, z])
                if z + 1 < nz:
                    total += apply_block(vecs[slot, place[z + 1], x, y], blocks[2, x, y, z])
                if z > 0:
                    total += apply_transposed(vecs[slot, place[z - 1], x, y], blocks[2, x, y, z - 1])
                acc[i, x, y] = total - center_shift * v.astype(F32)

    def whole(slot, i, z, x, y):
        total = acc[i, x, y]
        if x == nx - 1:
            total += apply_block(above_x[slot, i, y], blocks[0, x, y, z])
        if x == 0:
            total += below_x[slot, i, y].astype(F32)
        if y == ny - 1:
            total += apply_block(above_y[slot, i, x], blocks[1, x, y, z])
        if y == 0:
            total += below_y[slot, i, x].astype(F32)
        if z == nz - 1:
            total += apply_block(above_z[slot, x, y], blocks[2, x, y, z])
        if z == 0:
            total += below_z[slot, x, y].astype(F32)
        return total

    barrier = pltpu.get_barrier_semaphore()
    count = jnp.int32(0)
    for d in range(3):
        for way, there in ((1, has_up[d]), (-1, has_down[d])):
            pl.when(there)(functools.partial(
                pl.semaphore_signal, barrier, inc=1,
                device_id={AXES[d]: me[d] + way}, device_id_type=MESH))
            count += there.astype(jnp.int32)

    for d, (above, below) in enumerate(((above_x, below_x), (above_y, below_y), (above_z, below_z))):
        @pl.when(jnp.logical_not(has_up[d]))
        def _():
            above[...] = jnp.zeros_like(above)

        @pl.when(jnp.logical_not(has_down[d]))
        def _():
            below[...] = jnp.zeros_like(below)

    for i, z in enumerate(order):
        for x in range(nx):
            for y in range(ny):
                vecs[0, i, x, y] = trial[x, y, z]
                vecs[1, i, x, y] = jnp.zeros(trial.shape[3:], BF16)
                for d in range(3):
                    bond = bonds[d, x, y, z].astype(F32)
                    blocks[d, x, y, z] = (coupling[d, x, y, z].astype(F32) * bond).astype(BF16)

    pl.semaphore_wait(barrier, count)
    for chunk in range(len(chunks)):
        start(0, chunk, -1)
        partials(0, chunk)
        start(0, chunk, 1)

    def step(k, carry):
        slot = lax.rem(k, 2)
        other = 1 - slot
        scale = jnp.where(k == 0, half_inverse, 1.0)
        keep = jnp.where(k == 0, 0.0, 1.0)
        local_terms(slot)
        for chunk in range(len(chunks)):
            finish(slot, chunk)
            for i, z, x, y in cells(chunk):
                before = vecs[other, i, x, y].astype(F32)
                vecs[other, i, x, y] = (scale * whole(slot, i, z, x, y) - keep * before).astype(BF16)
            start(other, chunk, -1)
            partials(other, chunk)
            start(other, chunk, 1)
        return carry

    lax.fori_loop(0, STEPS - 1, step, 0)
    slot = (STEPS - 1) % 2
    local_terms(slot)
    for chunk in range(len(chunks)):
        finish(slot, chunk)
        for i, z, x, y in cells(chunk):
            out[x, y, z] = whole(slot, i, z, x, y) - vecs[1 - slot, i, x, y].astype(F32)


def shards(sizes, trial, onsite, coupling, bonds):
    nx, ny, nz, k, q = trial.shape
    vmem = pl.BlockSpec(memory_space=pltpu.VMEM)
    smem = pl.BlockSpec(memory_space=pltpu.SMEM)
    faces = [(2, nz, ny, k, q), (2, nz, nx, k, q), (2, nx, ny, k, q)]
    return pl.pallas_call(
        functools.partial(kernel, sizes),
        out_shape=jax.ShapeDtypeStruct(trial.shape, F32),
        in_specs=[smem, vmem, vmem, vmem],
        out_specs=vmem,
        scratch_shapes=[
            pltpu.VMEM((2, nz, nx, ny, k, q), BF16),
            pltpu.VMEM(coupling.shape, BF16),
            pltpu.VMEM((nz, nx, ny, k, q), F32),
            *[pltpu.VMEM(f, BF16) for f in faces],
            *[pltpu.VMEM(f, BF16) for f in faces],
            *[pltpu.VMEM(f, BF16) for f in faces],
            pltpu.SemaphoreType.DMA((2, 2, 6)),
            pltpu.SemaphoreType.DMA((2, 2, 6)),
        ],
        compiler_params=pltpu.CompilerParams(
            collective_id=0, has_side_effects=True, vmem_limit_bytes=32 * 1024 * 1024),
    )(bonds, trial, onsite, coupling)


def solution(mesh):
    placed = (
        P("gx", "gy", "gz", None, None),
        P("gx", "gy", "gz", None, None),
        P(None, "gx", "gy", "gz", None, None),
        P(None, "gx", "gy", "gz"),
    )
    return jax.shard_map(
        functools.partial(shards, tuple(mesh.shape[a] for a in AXES)),
        mesh=mesh,
        in_specs=placed,
        out_specs=P("gx", "gy", "gz", None, None),
        check_vma=False,
    )
```

time: 120 us -> 31.3 us (0.26)
  starting transfers between devices: 83.1 us -> 0 us
  Pallas kernels: 0 us -> 26.1 us
  matrix products: 17.1 us -> 0 us
  waiting for transfers between devices: 11.8 us -> 0 us
  other arithmetic: 4.45 us -> 0 us
  local copies, waits for them, and re-layouts: 1.26 us -> 4.88 us
    ppermute x30 -> x0, starting transfers between devices: 83.1 us -> none  [passed_along(): return lax.ppermute(block, axis, route)]
    pallas_call x0 -> x1, Pallas kernels: none -> 26.1 us  [shards(): pl.pallas_call(functools.partial(kernel, sizes), out_shape=jax.ShapeDtype...]
    dot_general x65 -> x0, matrix products: 17.1 us -> none  [the longest x35 10.9 us: block_apply(): jnp.einsum('...pq,...kq->...kp', blocks, vecs, preferred_element_type=jnp...]
    ppermute x30 -> x0, waiting for transfers between devices: 11.8 us -> none  [passed_along(): return lax.ppermute(block, axis, route)]
    unnamed x6 -> x9, local copies, waits for them, and re-layouts: 0.02 us -> 4.88 us
    mul x1 -> x0, other arithmetic: 1.62 us -> none  [shards(): blocks = coupling * bonds.astype(jnp.bfloat16)[..., None, None]]
  transfers between devices with their start and end apart: 30 -> 0, of which waited for: 6 -> 0; matrix products, arithmetic and copies ran while one was open for 9% -> 0% of each run, Pallas kernels for 0% -> 0%
where the time goes in v1:
time: 31.3 us; the launch traced here: 31 us
  Pallas kernels  26.1 us (83%)
  local copies, waits for them, and re-layouts  4.88 us (16%)
    pallas_call x1, Pallas kernels, shards(): pl.pallas_call(functools.partial(kernel, sizes), out_shape=jax.ShapeDtype...  26.1 us
    unnamed x9, local copies, waits for them, and re-layouts  4.88 us

profile of v1, /device:TPU:0, one launch (start us, length us, event | category | flops | bytes accessed | tf_op | source)
XLA Modules:
  0.0 31.0 jit_solution(14406724249466685884)
XLA Ops:
  0.0 0.0 copy-start
  0.0 1.4 %copy-done = bf16[3,2,2,4,128,128]{5,4,3,2,1,0:T(8,128)(2,1)S(1)} copy-done((bf16[3,2,2,4,128,128]{5,4,3,2,1,0:T(8,128)(2,1)S(1)}, bf16[3,2,2,4,128,128]{5,4,3,2,1,0:T(8,128)(2,1)}, u32[]{:S(2)}) %copy-start) | copy-done | bytes 1572888
  1.4 0.0 copy-start.1
  1.4 1.0 %copy-done.1 = bf16[2,2,4,128,128]{4,3,2,1,0:T(8,128)(2,1)S(1)} copy-done((bf16[2,2,4,128,128]{4,3,2,1,0:T(8,128)(2,1)S(1)}, bf16[2,2,4,128,128]{4,3,2,1,0:T(8,128)(2,1)}, u32[]{:S(2)}) %copy-start.1) | copy-done | bytes 524312
  2.5 0.0 copy-start.2
  2.5 0.9 %copy-done.2 = bf16[2,2,4,64,128]{4,3,2,1,0:T(8,128)(2,1)S(1)} copy-done((bf16[2,2,4,64,128]{4,3,2,1,0:T(8,128)(2,1)S(1)}, bf16[2,2,4,64,128]{4,3,2,1,0:T(8,128)(2,1)}, u32[]{:S(2)}) %copy-start.2) | copy-done | bytes 262168
  3.4 0.0 copy-start.3
  3.4 0.7 %copy-done.3 = s32[3,2,2,4]{3,2,1,0:T(2,128)S(1)} copy-done((s32[3,2,2,4]{3,2,1,0:T(2,128)S(1)}, s32[3,2,2,4]{3,2,1,0:T(2,128)}, u32[]{:S(2)}) %copy-start.3) | copy-done | bytes 216
  4.1 26.1 %shard_map.46 = f32[2,2,4,64,128]{4,3,2,1,0:T(8,128)S(1)} custom-call(s32[3,2,2,4]{3,2,1,0:T(2,128)S(1)} %copy-done.3, bf16[2,2,4,64,128]{4,3,2,1,0:T(8,128)(2,1)S(1)} %copy-done.2, bf16[2,2,4,128,128]{4,3,2,1,0:T(8,128)(2,1)S(1)} %copy-done.1, bf16[3,2,2,4,128,128]{5,4,3,2,1,0:T(8,128)(2,1)S(1)} %copy-done), custom_call_target="tpu_custom_call" | custom-call | tf_op jit(solution)/shard_map/pallas_call | solution.py:188
  30.2 0.8 %copy.6 = f32[2,2,4,64,128]{4,3,2,1,0:T(8,128)} copy(f32[2,2,4,64,128]{4,3,2,1,0:T(8,128)S(1)} %shard_map.46) | data formatting | bytes 1048576
Async XLA Ops:
  0.0 1.4 %copy-start = (bf16[3,2,2,4,128,128]{5,4,3,2,1,0:T(8,128)(2,1)S(1)}, bf16[3,2,2,4,128,128]{5,4,3,2,1,0:T(8,128)(2,1)}, u32[]{:S(2)}) copy-start(bf16[3,2,2,4,128,128]{5,4,3,2,1,0:T(8,128)(2,1)} %coupling.1) | copy-start | bytes 4718596
  1.4 1.0 %copy-start.1 = (bf16[2,2,4,128,128]{4,3,2,1,0:T(8,128)(2,1)S(1)}, bf16[2,2,4,128,128]{4,3,2,1,0:T(8,128)(2,1)}, u32[]{:S(2)}) copy-start(bf16[2,2,4,128,128]{4,3,2,1,0:T(8,128)(2,1)} %onsite.1) | copy-start | bytes 1572868
  2.5 0.9 %copy-start.2 = (bf16[2,2,4,64,128]{4,3,2,1,0:T(8,128)(2,1)S(1)}, bf16[2,2,4,64,128]{4,3,2,1,0:T(8,128)(2,1)}, u32[]{:S(2)}) copy-start(bf16[2,2,4,64,128]{4,3,2,1,0:T(8,128)(2,1)} %trial.1) | copy-start | bytes 786436
  3.4 0.7 %copy-start.3 = (s32[3,2,2,4]{3,2,1,0:T(2,128)S(1)}, s32[3,2,2,4]{3,2,1,0:T(2,128)}, u32[]{:S(2)}) copy-start(s32[3,2,2,4]{3,2,1,0:T(2,128)} %bonds.1) | copy-start | bytes 580

commit v2 on v1

v2 whole, which is shorter than its diff:
```python
import functools

import jax
import jax.numpy as jnp
from jax import lax
from jax.experimental import pallas as pl
from jax.experimental.pallas import tpu as pltpu
from jax.sharding import PartitionSpec as P

STEPS = 5

center_shift = 0.25
half_inverse = 0.5

BF16 = jnp.bfloat16
F32 = jnp.float32
MESH = pl.DeviceIdType.MESH
AXES = ("gx", "gy", "gz")


def product(vec, block):
    return lax.dot_general(vec, block, (((1,), (0,)), ((), ())), preferred_element_type=F32)


def side_by_side(parts):
    return parts[0] if len(parts) == 1 else jnp.concatenate(parts, axis=1)


def kernel(sizes, planes, bonds_in, trial, onsite, coupling, out, bonds, vecs, raw, acc,
           with_y, with_near, with_above, for_parts,
           above_x, above_y, above_z, below_x, below_y, below_z,
           part_x, part_y, part_z, send_sem, recv_sem, load_sem):
    nx, ny, nz, rows, q = trial.shape
    order = [0, nz - 1] + list(range(1, nz - 1)) if nz > 1 else [0]
    place = {z: i for i, z in enumerate(order)}
    chunks = [(lo, min(lo + planes, nz)) for lo in range(0, nz, planes)]
    length = (nx, ny, nz)

    me = [lax.axis_index(a) for a in AXES]
    has_up = [me[d] < sizes[d] - 1 for d in range(3)]
    has_down = [me[d] > 0 for d in range(3)]

    def near(z, x, y):
        here = (x, y, z)
        found = []
        for d in (0, 2):
            for way in (-1, 1):
                there = list(here)
                there[d] += way
                if 0 <= there[d] < length[d]:
                    found.append((d, way, tuple(there)))
        return found

    def tops(z, x, y):
        here = (x, y, z)
        return [d for d in range(3) if here[d] == length[d] - 1]

    def copies(slot, chunk):
        lo, hi = chunks[chunk]
        zs = pl.ds(lo, hi - lo)
        result = []

        def add(i, d, way, src, dst):
            def make():
                return pltpu.make_async_remote_copy(
                    src_ref=src, dst_ref=dst,
                    send_sem=send_sem.at[slot, chunk, i], recv_sem=recv_sem.at[slot, chunk, i],
                    device_id={AXES[d]: me[d] + way}, device_id_type=MESH)
            sends = has_up[d] if way > 0 else has_down[d]
            receives = has_down[d] if way > 0 else has_up[d]
            result.append((i, make, sends, receives))

        add(0, 1, -1, vecs.at[slot, zs, :, 0], above_y.at[slot, zs])
        add(1, 1, 1, part_y.at[slot, zs], below_y.at[slot, zs])
        if lo <= place[0] < hi:
            add(2, 2, -1, vecs.at[slot, place[0]], above_z.at[slot])
        if lo <= place[nz - 1] < hi:
            add(3, 2, 1, part_z.at[slot], below_z.at[slot])
        add(4, 0, -1, vecs.at[slot, zs, 0], above_x.at[slot, zs])
        add(5, 0, 1, part_x.at[slot, zs], below_x.at[slot, zs])
        return result

    def start(slot, chunk, ways):
        for i, make, sends, _ in copies(slot, chunk):
            if i % 2 in ways:
                @pl.when(sends)
                def _():
                    make().start()

    def receive(slot, chunk):
        lo, hi = chunks[chunk]
        for other in range(len(chunks)):
            for i, make, sends, receives in copies(slot, other):
                if (i == 2 and lo <= place[nz - 1] < hi) or (i == 3 and lo <= place[0] < hi) or (
                        i not in (2, 3) and other == chunk):
                    @pl.when(sends)
                    def _():
                        make().wait_send()

                    @pl.when(receives)
                    def _():
                        make().wait_recv()

    def cells(chunk):
        lo, hi = chunks[chunk]
        return [(i, order[i], x, y) for i in range(lo, hi) for x in range(nx) for y in range(ny)]

    def partials(slot, chunk):
        for i, z, x, y in cells(chunk):
            dims = tops(z, x, y)
            if not dims:
                continue
            sums = product(vecs[slot, i, x, y], for_parts[i, x, y, :, pl.ds(0, len(dims) * q)]).astype(BF16)
            for n, d in enumerate(dims):
                part = sums[:, n * q:(n + 1) * q]
                if d == 0:
                    part_x[slot, i, y] = part
                elif d == 1:
                    part_y[slot, i, x] = part
                else:
                    part_z[slot, x, y] = part

    def local_terms(slot):
        for i, z in enumerate(order):
            for x in range(nx):
                line = product(side_by_side([vecs[slot, i, x, y] for y in range(ny)]), with_y[i, x])
                for y in range(ny):
                    total = line[:, y * q:(y + 1) * q]
                    others = near(z, x, y)
                    if others:
                        total += product(
                            side_by_side([vecs[slot, place[c[2]], c[0], c[1]] for _, _, c in others]),
                            with_near[i, x, y, pl.ds(0, len(others) * q)])
                    acc[i, x, y] = total - center_shift * vecs[slot, i, x, y].astype(F32)

    def whole(slot, i, z, x, y):
        total = acc[i, x, y]
        dims = tops(z, x, y)
        if dims:
            given = {0: lambda: above_x[slot, i, y], 1: lambda: above_y[slot, i, x], 2: lambda: above_z[slot, x, y]}
            total += product(side_by_side([given[d]() for d in dims]), with_above[i, x, y, pl.ds(0, len(dims) * q)])
        if x == 0:
            total += below_x[slot, i, y].astype(F32)
        if y == 0:
            total += below_y[slot, i, x].astype(F32)
        if z == 0:
            total += below_z[slot, x, y].astype(F32)
        return total

    def masked(d, i, z, x, y):
        return (raw[i, d, x, y].astype(F32) * bonds[d, x, y, z].astype(F32)).astype(BF16)

    barrier = pltpu.get_barrier_semaphore()
    count = jnp.int32(0)
    for d in range(3):
        for way, there in ((1, has_up[d]), (-1, has_down[d])):
            pl.when(there)(functools.partial(
                pl.semaphore_signal, barrier, inc=1,
                device_id={AXES[d]: me[d] + way}, device_id_type=MESH))
            count += there.astype(jnp.int32)

    loads_vec = [pltpu.make_async_copy(trial.at[:, :, z], vecs.at[0, i], load_sem.at[0, i])
                 for i, z in enumerate(order)]
    load_bonds = pltpu.make_async_copy(bonds_in, bonds, load_sem.at[2, 0])
    loads_block = [pltpu.make_async_copy(coupling.at[:, :, :, z], raw.at[i], load_sem.at[1, i])
                   for i, z in enumerate(order)]
    loads_site = [[pltpu.make_async_copy(
        onsite.at[:, y, z], with_y.at[i, :, pl.ds(y * q, q), pl.ds(y * q, q)], load_sem.at[3 + y, i])
        for y in range(ny)] for i, z in enumerate(order)]
    for copy in loads_vec + [load_bonds] + loads_block + sum(loads_site, []):
        copy.start()

    for d, (above, below) in enumerate(((above_x, below_x), (above_y, below_y), (above_z, below_z))):
        @pl.when(jnp.logical_not(has_up[d]))
        def _():
            above[...] = jnp.zeros_like(above)

        @pl.when(jnp.logical_not(has_down[d]))
        def _():
            below[...] = jnp.zeros_like(below)

    vecs[1] = jnp.zeros(vecs.shape[1:], BF16)
    if ny > 2:
        for i in range(nz):
            for x in range(nx):
                for y in range(ny):
                    for other in range(ny):
                        if abs(other - y) > 1:
                            with_y[i, x, pl.ds(y * q, q), pl.ds(other * q, q)] = jnp.zeros((q, q), BF16)

    pl.semaphore_wait(barrier, count)
    for copy in loads_vec:
        copy.wait()
    for chunk in range(len(chunks)):
        start(0, chunk, (0,))
    load_bonds.wait()
    for chunk in range(len(chunks)):
        for i in range(*chunks[chunk]):
            loads_block[i].wait()
        for i, z, x, y in cells(chunk):
            for n, d in enumerate(tops(z, x, y)):
                for_parts[i, x, y, :, pl.ds(n * q, q)] = masked(d, i, z, x, y)
        partials(0, chunk)
        start(0, chunk, (1,))
    for chunk in range(len(chunks)):
        for i, z, x, y in cells(chunk):
            here = (x, y, z)
            dims = tops(z, x, y)
            for d in range(3):
                if d in dims:
                    n = dims.index(d)
                    with_above[i, x, y, pl.ds(n * q, q)] = for_parts[i, x, y, :, pl.ds(n * q, q)].T
                    continue
                block = masked(d, i, z, x, y)
                if d == 1:
                    with_y[i, x, pl.ds(y * q, q), pl.ds((y + 1) * q, q)] = block
                    with_y[i, x, pl.ds((y + 1) * q, q), pl.ds(y * q, q)] = block.T
                    continue
                there = list(here)
                there[d] += 1
                up = [(e, way) for e, way, _ in near(z, x, y)].index((d, 1))
                down = [(e, way) for e, way, _ in near(there[2], there[0], there[1])].index((d, -1))
                with_near[i, x, y, pl.ds(up * q, q)] = block.T
                with_near[place[there[2]], there[0], there[1], pl.ds(down * q, q)] = block
    for copy in sum(loads_site, []):
        copy.wait()

    def step(k, carry):
        slot = lax.rem(k, 2)
        other = 1 - slot
        scale = jnp.where(k == 0, half_inverse, 1.0)
        keep = jnp.where(k == 0, 0.0, 1.0)
        local_terms(slot)
        for chunk in range(len(chunks)):
            receive(slot, chunk)
            for i, z, x, y in cells(chunk):
                before = vecs[other, i, x, y].astype(F32)
                vecs[other, i, x, y] = (scale * whole(slot, i, z, x, y) - keep * before).astype(BF16)
            start(other, chunk, (0,))
            partials(other, chunk)
            start(other, chunk, (1,))
        return carry

    lax.fori_loop(0, STEPS - 1, step, 0)
    slot = (STEPS - 1) % 2
    local_terms(slot)
    for chunk in range(len(chunks)):
        receive(slot, chunk)
        for i, z, x, y in cells(chunk):
            out[x, y, z] = whole(slot, i, z, x, y) - vecs[1 - slot, i, x, y].astype(F32)


def shards(sizes, trial, onsite, coupling, bonds):
    nx, ny, nz, k, q = trial.shape
    planes = 1
    hbm = pl.BlockSpec(memory_space=pltpu.HBM)
    faces = [(2, nz, ny, k, q), (2, nz, nx, k, q), (2, nx, ny, k, q)]
    return pl.pallas_call(
        functools.partial(kernel, sizes, planes),
        out_shape=jax.ShapeDtypeStruct(trial.shape, F32),
        in_specs=[hbm, hbm, hbm, hbm],
        out_specs=pl.BlockSpec(memory_space=pltpu.VMEM),
        scratch_shapes=[
            pltpu.SMEM(bonds.shape, jnp.int32),
            pltpu.VMEM((2, nz, nx, ny, k, q), BF16),
            pltpu.VMEM((nz, 3, nx, ny, q, q), BF16),
            pltpu.VMEM((nz, nx, ny, k, q), F32),
            pltpu.VMEM((nz, nx, ny * q, ny * q), BF16),
            pltpu.VMEM((nz, nx, ny, 4 * q, q), BF16),
            pltpu.VMEM((nz, nx, ny, 3 * q, q), BF16),
            pltpu.VMEM((nz, nx, ny, q, 3 * q), BF16),
            *[pltpu.VMEM(f, BF16) for f in faces],
            *[pltpu.VMEM(f, BF16) for f in faces],
            *[pltpu.VMEM(f, BF16) for f in faces],
            pltpu.SemaphoreType.DMA((2, nz, 6)),
            pltpu.SemaphoreType.DMA((2, nz, 6)),
            pltpu.SemaphoreType.DMA((3 + ny, nz)),
        ],
        compiler_params=pltpu.CompilerParams(
            collective_id=0, has_side_effects=True, vmem_limit_bytes=48 * 1024 * 1024),
    )(bonds, trial, onsite, coupling)


def solution(mesh):
    placed = (
        P("gx", "gy", "gz", None, None),
        P("gx", "gy", "gz", None, None),
        P(None, "gx", "gy", "gz", None, None),
        P(None, "gx", "gy", "gz"),
    )
    return jax.shard_map(
        functools.partial(shards, tuple(mesh.shape[a] for a in AXES)),
        mesh=mesh,
        in_specs=placed,
        out_specs=P("gx", "gy", "gz", None, None),
        check_vma=False,
    )
```

time: 31.3 us -> 28.8 us (0.920)
  Pallas kernels: 26.1 us -> 23.6 us
    pallas_call x1, Pallas kernels: 26.1 us -> 23.6 us  [shards(): pl.pallas_call(functools.partial(kernel, sizes, planes), out_shape=jax.Sh...]
where the time goes in v2:
time: 28.8 us; the launch traced here: 28.5 us
  Pallas kernels  23.6 us (82%)
  local copies, waits for them, and re-layouts  4.88 us (17%)
    pallas_call x1, Pallas kernels, shards(): pl.pallas_call(functools.partial(kernel, sizes, planes), out_shape=jax.Sh...  23.6 us
    unnamed x9, local copies, waits for them, and re-layouts  4.88 us

profile of v2, /device:TPU:0, one launch (start us, length us, event | category | flops | bytes accessed | tf_op | source)
XLA Modules:
  0.0 28.5 jit_solution(1349509985226482698)
XLA Ops:
  0.0 0.0 copy-start
  0.0 1.4 %copy-done = bf16[3,2,2,4,128,128]{5,4,3,2,1,0:T(8,128)(2,1)S(1)} copy-done((bf16[3,2,2,4,128,128]{5,4,3,2,1,0:T(8,128)(2,1)S(1)}, bf16[3,2,2,4,128,128]{5,4,3,2,1,0:T(8,128)(2,1)}, u32[]{:S(2)}) %copy-start) | copy-done | bytes 1572888
  1.4 0.0 copy-start.1
  1.4 1.0 %copy-done.1 = bf16[2,2,4,128,128]{4,3,2,1,0:T(8,128)(2,1)S(1)} copy-done((bf16[2,2,4,128,128]{4,3,2,1,0:T(8,128)(2,1)S(1)}, bf16[2,2,4,128,128]{4,3,2,1,0:T(8,128)(2,1)}, u32[]{:S(2)}) %copy-start.1) | copy-done | bytes 524312
  2.5 0.0 copy-start.2
  2.5 0.9 %copy-done.2 = bf16[2,2,4,64,128]{4,3,2,1,0:T(8,128)(2,1)S(1)} copy-done((bf16[2,2,4,64,128]{4,3,2,1,0:T(8,128)(2,1)S(1)}, bf16[2,2,4,64,128]{4,3,2,1,0:T(8,128)(2,1)}, u32[]{:S(2)}) %copy-start.2) | copy-done | bytes 262168
  3.4 0.0 copy-start.3
  3.4 0.7 %copy-done.3 = s32[3,2,2,4]{3,2,1,0:T(2,128)S(1)} copy-done((s32[3,2,2,4]{3,2,1,0:T(2,128)S(1)}, s32[3,2,2,4]{3,2,1,0:T(2,128)}, u32[]{:S(2)}) %copy-start.3) | copy-done | bytes 216
  4.1 23.6 %shard_map.46 = f32[2,2,4,64,128]{4,3,2,1,0:T(8,128)S(1)} custom-call(s32[3,2,2,4]{3,2,1,0:T(2,128)S(1)} %copy-done.3, bf16[2,2,4,64,128]{4,3,2,1,0:T(8,128)(2,1)S(1)} %copy-done.2, bf16[2,2,4,128,128]{4,3,2,1,0:T(8,128)(2,1)S(1)} %copy-done.1, bf16[3,2,2,4,128,128]{5,4,3,2,1,0:T(8,128)(2,1)S(1)} %copy-done), custom_call_target="tpu_custom_call" | custom-call | tf_op jit(solution)/shard_map/pallas_call | solution.py:258
  27.7 0.8 %copy.6 = f32[2,2,4,64,128]{4,3,2,1,0:T(8,128)} copy(f32[2,2,4,64,128]{4,3,2,1,0:T(8,128)S(1)} %shard_map.46) | data formatting | bytes 1048576
Async XLA Ops:
  0.0 1.4 %copy-start = (bf16[3,2,2,4,128,128]{5,4,3,2,1,0:T(8,128)(2,1)S(1)}, bf16[3,2,2,4,128,128]{5,4,3,2,1,0:T(8,128)(2,1)}, u32[]{:S(2)}) copy-start(bf16[3,2,2,4,128,128]{5,4,3,2,1,0:T(8,128)(2,1)} %coupling.1) | copy-start | bytes 4718596
  1.4 1.0 %copy-start.1 = (bf16[2,2,4,128,128]{4,3,2,1,0:T(8,128)(2,1)S(1)}, bf16[2,2,4,128,128]{4,3,2,1,0:T(8,128)(2,1)}, u32[]{:S(2)}) copy-start(bf16[2,2,4,128,128]{4,3,2,1,0:T(8,128)(2,1)} %onsite.1) | copy-start | bytes 1572868
  2.5 0.9 %copy-start.2 = (bf16[2,2,4,64,128]{4,3,2,1,0:T(8,128)(2,1)S(1)}, bf16[2,2,4,64,128]{4,3,2,1,0:T(8,128)(2,1)}, u32[]{:S(2)}) copy-start(bf16[2,2,4,64,128]{4,3,2,1,0:T(8,128)(2,1)} %trial.1) | copy-start | bytes 786436
  3.4 0.7 %copy-start.3 = (s32[3,2,2,4]{3,2,1,0:T(2,128)S(1)}, s32[3,2,2,4]{3,2,1,0:T(2,128)}, u32[]{:S(2)}) copy-start(s32[3,2,2,4]{3,2,1,0:T(2,128)} %bonds_in.1) | copy-start | bytes 580

commit v3 on v2

--- a/solution.py
+++ b/solution.py
@@ -26,14 +26,14 @@
     return parts[0] if len(parts) == 1 else jnp.concatenate(parts, axis=1)
 
 
-def kernel(sizes, planes, bonds_in, trial, onsite, coupling, out, bonds, vecs, raw, acc,
+def kernel(sizes, bonds_in, trial, onsite, coupling, out, bonds, vecs, raw, acc,
            with_y, with_near, with_above, for_parts,
            above_x, above_y, above_z, below_x, below_y, below_z,
            part_x, part_y, part_z, send_sem, recv_sem, load_sem):
     nx, ny, nz, rows, q = trial.shape
     order = [0, nz - 1] + list(range(1, nz - 1)) if nz > 1 else [0]
     place = {z: i for i, z in enumerate(order)}
-    chunks = [(lo, min(lo + planes, nz)) for lo in range(0, nz, planes)]
+    chunks = [(i, i + 1) for i in range(nz)]
     length = (nx, ny, nz)
 
     me = [lax.axis_index(a) for a in AXES]
@@ -55,33 +55,33 @@
         here = (x, y, z)
         return [d for d in range(3) if here[d] == length[d] - 1]
 
-    def copies(slot, chunk):
-        lo, hi = chunks[chunk]
-        zs = pl.ds(lo, hi - lo)
+    def copies(slot, chunk, first=False):
+        i = chunk
+        z = order[i]
         result = []
 
-        def add(i, d, way, src, dst):
+        def add(kind, d, way, src, dst):
             def make():
                 return pltpu.make_async_remote_copy(
                     src_ref=src, dst_ref=dst,
-                    send_sem=send_sem.at[slot, chunk, i], recv_sem=recv_sem.at[slot, chunk, i],
+                    send_sem=send_sem.at[slot, chunk, kind], recv_sem=recv_sem.at[slot, chunk, kind],
                     device_id={AXES[d]: me[d] + way}, device_id_type=MESH)
             sends = has_up[d] if way > 0 else has_down[d]
             receives = has_down[d] if way > 0 else has_up[d]
-            result.append((i, make, sends, receives))
-
-        add(0, 1, -1, vecs.at[slot, zs, :, 0], above_y.at[slot, zs])
-        add(1, 1, 1, part_y.at[slot, zs], below_y.at[slot, zs])
-        if lo <= place[0] < hi:
-            add(2, 2, -1, vecs.at[slot, place[0]], above_z.at[slot])
-        if lo <= place[nz - 1] < hi:
+            result.append((kind, make, sends, receives))
+
+        add(0, 1, -1, trial.at[:, 0, z] if first else vecs.at[slot, i, :, 0], above_y.at[slot, i])
+        add(1, 1, 1, part_y.at[slot, i], below_y.at[slot, i])
+        if z == 0:
+            add(2, 2, -1, trial.at[:, :, z] if first else vecs.at[slot, i], above_z.at[slot])
+        if z == nz - 1:
             add(3, 2, 1, part_z.at[slot], below_z.at[slot])
-        add(4, 0, -1, vecs.at[slot, zs, 0], above_x.at[slot, zs])
-        add(5, 0, 1, part_x.at[slot, zs], below_x.at[slot, zs])
+        add(4, 0, -1, trial.at[0, :, z] if first else vecs.at[slot, i, 0], above_x.at[slot, i])
+        add(5, 0, 1, part_x.at[slot, i], below_x.at[slot, i])
         return result
 
-    def start(slot, chunk, ways):
-        for i, make, sends, _ in copies(slot, chunk):
+    def start(slot, chunk, ways, first=False):
+        for i, make, sends, _ in copies(slot, chunk, first):
             if i % 2 in ways:
                 @pl.when(sends)
                 def _():
@@ -161,13 +161,14 @@
 
     loads_vec = [pltpu.make_async_copy(trial.at[:, :, z], vecs.at[0, i], load_sem.at[0, i])
                  for i, z in enumerate(order)]
+    stores = [pltpu.make_async_copy(acc.at[i], out.at[:, :, z], load_sem.at[0, i]) for i, z in enumerate(order)]
     load_bonds = pltpu.make_async_copy(bonds_in, bonds, load_sem.at[2, 0])
     loads_block = [pltpu.make_async_copy(coupling.at[:, :, :, z], raw.at[i], load_sem.at[1, i])
                    for i, z in enumerate(order)]
     loads_site = [[pltpu.make_async_copy(
         onsite.at[:, y, z], with_y.at[i, :, pl.ds(y * q, q), pl.ds(y * q, q)], load_sem.at[3 + y, i])
         for y in range(ny)] for i, z in enumerate(order)]
-    for copy in loads_vec + [load_bonds] + loads_block + sum(loads_site, []):
+    for copy in [load_bonds] + loads_vec + loads_block + sum(loads_site, []):
         copy.start()
 
     for d, (above, below) in enumerate(((above_x, below_x), (above_y, below_y), (above_z, below_z))):
@@ -189,10 +190,10 @@
                             with_y[i, x, pl.ds(y * q, q), pl.ds(other * q, q)] = jnp.zeros((q, q), BF16)
 
     pl.semaphore_wait(barrier, count)
+    for chunk in range(len(chunks)):
+        start(0, chunk, (0,), first=True)
     for copy in loads_vec:
         copy.wait()
-    for chunk in range(len(chunks)):
-        start(0, chunk, (0,))
     load_bonds.wait()
     for chunk in range(len(chunks)):
         for i in range(*chunks[chunk]):
@@ -247,19 +248,22 @@
     for chunk in range(len(chunks)):
         receive(slot, chunk)
         for i, z, x, y in cells(chunk):
-            out[x, y, z] = whole(slot, i, z, x, y) - vecs[1 - slot, i, x, y].astype(F32)
+            acc[i, x, y] = whole(slot, i, z, x, y) - vecs[1 - slot, i, x, y].astype(F32)
+        for i in range(*chunks[chunk]):
+            stores[i].start()
+    for copy in stores:
+        copy.wait()
 
 
 def shards(sizes, trial, onsite, coupling, bonds):
     nx, ny, nz, k, q = trial.shape
-    planes = 1
     hbm = pl.BlockSpec(memory_space=pltpu.HBM)
     faces = [(2, nz, ny, k, q), (2, nz, nx, k, q), (2, nx, ny, k, q)]
     return pl.pallas_call(
-        functools.partial(kernel, sizes, planes),
+        functools.partial(kernel, sizes),
         out_shape=jax.ShapeDtypeStruct(trial.shape, F32),
         in_specs=[hbm, hbm, hbm, hbm],
-        out_specs=pl.BlockSpec(memory_space=pltpu.VMEM),
+        out_specs=hbm,
         scratch_shapes=[
             pltpu.SMEM(bonds.shape, jnp.int32),
             pltpu.VMEM((2, nz, nx, ny, k, q), BF16),
@@ -277,7 +281,7 @@
             pltpu.SemaphoreType.DMA((3 + ny, nz)),
         ],
         compiler_params=pltpu.CompilerParams(
-            collective_id=0, has_side_effects=True, vmem_limit_bytes=48 * 1024 * 1024),
+            collective_id=0, has_side_effects=True, vmem_limit_bytes=60 * 1024 * 1024),
     )(bonds, trial, onsite, coupling)
 
 

time: 28.8 us -> 26.6 us (0.924)
  local copies, waits for them, and re-layouts: 4.88 us -> 1.89 us
  Pallas kernels: 23.6 us -> 24.5 us
    unnamed x9 -> x1, local copies, waits for them, and re-layouts: 4.88 us -> 1.89 us
    pallas_call x1, Pallas kernels: 23.6 us -> 24.5 us  [shards(): pl.pallas_call(functools.partial(kernel, sizes), out_shape=jax.ShapeDtype...]
where the time goes in v3:
time: 26.6 us; the launch traced here: 26.4 us
  Pallas kernels  24.5 us (92%)
  local copies, waits for them, and re-layouts  1.89 us (7%)
    pallas_call x1, Pallas kernels, shards(): pl.pallas_call(functools.partial(kernel, sizes), out_shape=jax.ShapeDtype...  24.5 us
    unnamed x1, local copies, waits for them, and re-layouts  1.89 us

profile of v3, /device:TPU:0, one launch (start us, length us, event | category | flops | bytes accessed | tf_op | source)
XLA Modules:
  0.0 26.4 jit_solution(9428022160010144051)
XLA Ops:
  0.0 24.5 %shard_map.46 = f32[2,2,4,64,128]{4,3,2,1,0:T(8,128)} custom-call(s32[3,2,2,4]{3,2,1,0:T(2,128)} %bonds_in.1, bf16[2,2,4,64,128]{4,3,2,1,0:T(8,128)(2,1)} %trial.1, bf16[2,2,4,128,128]{4,3,2,1,0:T(8,128)(2,1)} %onsite.1, bf16[3,2,2,4,128,128]{5,4,3,2,1,0:T(8,128)(2,1)} %coupling.1), custom_call_target="tpu_custom_call" | custom-call | tf_op jit(solution)/shard_map/pallas_call | solution.py:262
  24.5 1.9 %copy.6 = f32[2,2,4,64,128]{4,3,2,1,0:T(8,128)} copy(f32[2,2,4,64,128]{4,3,2,1,0:T(8,128)} %shard_map.46) | data formatting | bytes 1048576

commit v4 on v3

--- a/solution.py
+++ b/solution.py
@@ -33,7 +33,7 @@
     nx, ny, nz, rows, q = trial.shape
     order = [0, nz - 1] + list(range(1, nz - 1)) if nz > 1 else [0]
     place = {z: i for i, z in enumerate(order)}
-    chunks = [(i, i + 1) for i in range(nz)]
+    chunks = [(i, x) for i in range(nz) for x in range(nx)]
     length = (nx, ny, nz)
 
     me = [lax.axis_index(a) for a in AXES]
@@ -56,7 +56,7 @@
         return [d for d in range(3) if here[d] == length[d] - 1]
 
     def copies(slot, chunk, first=False):
-        i = chunk
+        i, x = chunks[chunk]
         z = order[i]
         result = []
 
@@ -70,14 +70,16 @@
             receives = has_down[d] if way > 0 else has_up[d]
             result.append((kind, make, sends, receives))
 
-        add(0, 1, -1, trial.at[:, 0, z] if first else vecs.at[slot, i, :, 0], above_y.at[slot, i])
-        add(1, 1, 1, part_y.at[slot, i], below_y.at[slot, i])
+        add(0, 1, -1, trial.at[x, 0, z] if first else vecs.at[slot, i, x, 0], above_y.at[slot, i, x])
+        add(1, 1, 1, part_y.at[slot, i, x], below_y.at[slot, i, x])
         if z == 0:
-            add(2, 2, -1, trial.at[:, :, z] if first else vecs.at[slot, i], above_z.at[slot])
+            add(2, 2, -1, trial.at[x, :, z] if first else vecs.at[slot, i, x], above_z.at[slot, x])
         if z == nz - 1:
-            add(3, 2, 1, part_z.at[slot], below_z.at[slot])
-        add(4, 0, -1, trial.at[0, :, z] if first else vecs.at[slot, i, 0], above_x.at[slot, i])
-        add(5, 0, 1, part_x.at[slot, i], below_x.at[slot, i])
+            add(3, 2, 1, part_z.at[slot, x], below_z.at[slot, x])
+        if x == 0:
+            add(4, 0, -1, trial.at[0, :, z] if first else vecs.at[slot, i, 0], above_x.at[slot, i])
+        if x == nx - 1:
+            add(5, 0, 1, part_x.at[slot, i], below_x.at[slot, i])
         return result
 
     def start(slot, chunk, ways, first=False):
@@ -88,11 +90,19 @@
                     make().start()
 
     def receive(slot, chunk):
-        lo, hi = chunks[chunk]
-        for other in range(len(chunks)):
-            for i, make, sends, receives in copies(slot, other):
-                if (i == 2 and lo <= place[nz - 1] < hi) or (i == 3 and lo <= place[0] < hi) or (
-                        i not in (2, 3) and other == chunk):
+        i, x = chunks[chunk]
+        last = nz - 1
+        for other, (j, w) in enumerate(chunks):
+            for kind, make, sends, receives in copies(slot, other):
+                needed = {
+                    0: other == chunk,
+                    1: other == chunk,
+                    2: w == x and order[i] == last,
+                    3: w == x and order[i] == 0,
+                    4: j == i and x == nx - 1,
+                    5: j == i and x == 0,
+                }[kind]
+                if needed:
                     @pl.when(sends)
                     def _():
                         make().wait_send()
@@ -102,8 +112,8 @@
                         make().wait_recv()
 
     def cells(chunk):
-        lo, hi = chunks[chunk]
-        return [(i, order[i], x, y) for i in range(lo, hi) for x in range(nx) for y in range(ny)]
+        i, x = chunks[chunk]
+        return [(i, order[i], x, y) for y in range(ny)]
 
     def partials(slot, chunk):
         for i, z, x, y in cells(chunk):
@@ -196,8 +206,8 @@
         copy.wait()
     load_bonds.wait()
     for chunk in range(len(chunks)):
-        for i in range(*chunks[chunk]):
-            loads_block[i].wait()
+        if chunks[chunk][1] == 0:
+            loads_block[chunks[chunk][0]].wait()
         for i, z, x, y in cells(chunk):
             for n, d in enumerate(tops(z, x, y)):
                 for_parts[i, x, y, :, pl.ds(n * q, q)] = masked(d, i, z, x, y)
@@ -249,8 +259,8 @@
         receive(slot, chunk)
         for i, z, x, y in cells(chunk):
             acc[i, x, y] = whole(slot, i, z, x, y) - vecs[1 - slot, i, x, y].astype(F32)
-        for i in range(*chunks[chunk]):
-            stores[i].start()
+        if chunks[chunk][1] == nx - 1:
+            stores[chunks[chunk][0]].start()
     for copy in stores:
         copy.wait()
 
@@ -276,8 +286,8 @@
             *[pltpu.VMEM(f, BF16) for f in faces],
             *[pltpu.VMEM(f, BF16) for f in faces],
             *[pltpu.VMEM(f, BF16) for f in faces],
-            pltpu.SemaphoreType.DMA((2, nz, 6)),
-            pltpu.SemaphoreType.DMA((2, nz, 6)),
+            pltpu.SemaphoreType.DMA((2, nz * nx, 6)),
+            pltpu.SemaphoreType.DMA((2, nz * nx, 6)),
             pltpu.SemaphoreType.DMA((3 + ny, nz)),
         ],
         compiler_params=pltpu.CompilerParams(

time: 26.6 us -> 26.2 us (0.985)
  Pallas kernels: 24.5 us -> 24.1 us
    pallas_call x1, Pallas kernels: 24.5 us -> 24.1 us  [shards(): pl.pallas_call(functools.partial(kernel, sizes), out_shape=jax.ShapeDtype...]
where the time goes in v4:
time: 26.2 us; the launch traced here: 26 us
  Pallas kernels  24.1 us (92%)
  local copies, waits for them, and re-layouts  1.89 us (7%)
    pallas_call x1, Pallas kernels, shards(): pl.pallas_call(functools.partial(kernel, sizes), out_shape=jax.ShapeDtype...  24.1 us
    unnamed x1, local copies, waits for them, and re-layouts  1.89 us

profile of v4, /device:TPU:0, one launch (start us, length us, event | category | flops | bytes accessed | tf_op | source)
XLA Modules:
  0.0 26.0 jit_solution(3001697076380020466)
XLA Ops:
  0.0 24.1 %shard_map.46 = f32[2,2,4,64,128]{4,3,2,1,0:T(8,128)} custom-call(s32[3,2,2,4]{3,2,1,0:T(2,128)} %bonds_in.1, bf16[2,2,4,64,128]{4,3,2,1,0:T(8,128)(2,1)} %trial.1, bf16[2,2,4,128,128]{4,3,2,1,0:T(8,128)(2,1)} %onsite.1, bf16[3,2,2,4,128,128]{5,4,3,2,1,0:T(8,128)(2,1)} %coupling.1), custom_call_target="tpu_custom_call" | custom-call | tf_op jit(solution)/shard_map/pallas_call | solution.py:272
  24.1 1.9 %copy.6 = f32[2,2,4,64,128]{4,3,2,1,0:T(8,128)} copy(f32[2,2,4,64,128]{4,3,2,1,0:T(8,128)} %shard_map.46) | data formatting | bytes 1048576
